TPU v7x, 512 devices: a whole 4x8x8 slice. The times are simulated.
512 devices in a mesh: batch: 16 (over z, core), ctx: 32 (over y, x).
Axes of the slice: x: 4, y: 8, z: 8, core: 2. Of those that a mesh axis runs over, the one named last changes fastest.
Arguments:
- q_latent: bfloat16 [4, 32, 64, 512], P(None, 'ctx', 'batch'), may hold values from -48 to 48
- q_rope: bfloat16 [4, 32, 64, 64], P(None, 'ctx', 'batch'), may hold values from -3 to 3
- cache_latent: bfloat16 [32, 32768, 512], P('batch', 'ctx'), may hold values from -6 to 6, as said below
- cache_rope: bfloat16 [32, 32768, 64], P('batch', 'ctx'), may hold values from -6 to 6
- new_latent: bfloat16 [4, 32, 512], P(None, 'batch'), may hold values from -6 to 6, as said below
- new_rope: bfloat16 [4, 32, 64], P(None, 'batch'), may hold values from -6 to 6
- lengths: int32 [32], P('batch'), may hold values from 8192 to 32768, as said below
- selected: int32 [4, 32, 8, 3], P(None, 'batch'), may hold values from 0 to 63, as said below
- w_uv: bfloat16 [64, 512, 128], P('batch'), may hold values from -2 to 2
Outputs:
- attended: bfloat16 [4, 32, 64, 128], P(None, None, 'batch')
Inputs may be any that keep to these rules, and one draw needn't show every extreme that they name: `lengths`: filled positions of one request; one request is full and one holds exactly 8192. `selected`: the 3 ids of one row are distinct block ids, each below ceil(lengths[r] / 512); every row holds block 0 and the request's last filled block. `new_latent`: Real-valued latent entries. `cache_latent`: Real-valued latent entries.
All inputs are finite; a program needn't handle non-finite values.
Results may differ from a plain program's by a relative error of at most 0.0059.
Values may be sent and summed in bfloat16 or wider, within the bound.
A program may use at most 128 MiB of HBM per device.

v0:
```python
import jax
import jax.numpy as jnp
from jax import lax
from jax.sharding import PartitionSpec as P

KR = 64
VH = 128
BLOCK = 512


def combined_all(value, axis, combine):
    everything = jax.tree.map(lambda part: lax.all_gather(part, axis), value)
    leading = jax.tree.map(lambda part: part[0], everything)

    def lap(k, so_far):
        return combine(so_far, jax.tree.map(lambda part: part[k], everything))

    return lax.fori_loop(1, lax.axis_size(axis), lap, leading)


def combine(first_state, second_state):
    first_max, first_sum, first_out = first_state
    second_max, second_sum, second_out = second_state
    joint_max = jnp.maximum(first_max, second_max)
    first_factor = jnp.exp(first_max - joint_max)
    second_factor = jnp.exp(second_max - joint_max)
    joint_sum = first_sum * first_factor + second_sum * second_factor
    joint_out = first_out * first_factor[..., None] + second_out * second_factor[..., None]
    return (joint_max, joint_sum, joint_out)


def local_partials(q_lat, q_rot, cache_latent, cache_rope, lengths, selected):
    step_count, req_count, head_count, row_width = q_lat.shape
    blocks_dev = cache_latent.shape[1] // BLOCK
    groups = selected.shape[2]
    per_group = head_count // groups
    scale = (VH + KR) ** (-0.5)
    first_block = lax.axis_index("ctx") * blocks_dev
    init_state = (
        jnp.full((step_count, req_count, head_count), -1e30, jnp.float32),
        jnp.zeros((step_count, req_count, head_count), jnp.float32),
        jnp.zeros((step_count, req_count, head_count, row_width), jnp.float32),
    )

    def visit_item(item_index, run_state):
        request = item_index // blocks_dev
        local_block = item_index % blocks_dev
        global_block = first_block + local_block
        chosen_ids = lax.dynamic_index_in_dim(selected, request, 1, keepdims=False)
        chosen = jnp.any(chosen_ids == global_block, axis=-1)

        def attend(state):
            run_max, run_sum, run_out = state
            lat_query = lax.dynamic_index_in_dim(q_lat, request, 1, keepdims=False)
            rot_query = lax.dynamic_index_in_dim(q_rot, request, 1, keepdims=False)
            lat_rows = lax.dynamic_slice_in_dim(
                lax.dynamic_index_in_dim(cache_latent, request, 0, keepdims=False),
                local_block * BLOCK,
                BLOCK,
                0,
            )
            rot_rows = lax.dynamic_slice_in_dim(
                lax.dynamic_index_in_dim(cache_rope, request, 0, keepdims=False),
                local_block * BLOCK,
                BLOCK,
                0,
            )
            scores = jnp.einsum(
                "shd,jd->shj", lat_query, lat_rows, preferred_element_type=jnp.float32
            )
            scores = (
                scores
                + jnp.einsum("shd,jd->shj", rot_query, rot_rows, preferred_element_type=jnp.float32)
            ) * scale
            length = lengths[request]
            position = global_block * BLOCK + jnp.arange(BLOCK, dtype=jnp.int32)
            keep_mask = (
                jnp.repeat(chosen, per_group, axis=1)[:, :, None]
                & (position < length)[None, None, :]
            )
            scores = jnp.where(keep_mask, scores, -1e30)
            old_max = lax.dynamic_index_in_dim(run_max, request, 1, keepdims=False)
            old_sum = lax.dynamic_index_in_dim(run_sum, request, 1, keepdims=False)
            old_out = lax.dynamic_index_in_dim(run_out, request, 1, keepdims=False)
            new_max = jnp.maximum(old_max, jnp.max(scores, axis=-1))
            weights = jnp.where(keep_mask, jnp.exp(scores - new_max[..., None]), 0.0)
            factor = jnp.exp(old_max - new_max)
            new_sum = old_sum * factor + jnp.sum(weights, axis=-1)
            new_out = old_out * factor[..., None] + jnp.einsum(
                "shj,jd->shd",
                weights.astype(jnp.bfloat16),
                lat_rows,
                preferred_element_type=jnp.float32,
            )
            return (
                lax.dynamic_update_index_in_dim(run_max, new_max, request, 1),
                lax.dynamic_update_index_in_dim(run_sum, new_sum, request, 1),
                lax.dynamic_update_index_in_dim(run_out, new_out, request, 1),
            )

        return lax.cond(jnp.any(chosen), attend, lambda state: state, run_state)

    return lax.fori_loop(0, req_count * blocks_dev, visit_item, init_state)


def finish(q_lat, q_rot, run_max, run_sum, run_out, new_latent, new_rope):
    step_count = q_lat.shape[0]
    scale = (VH + KR) ** (-0.5)
    scores = jnp.einsum("srhd,urd->srhu", q_lat, new_latent, preferred_element_type=jnp.float32)
    scores = (
        scores + jnp.einsum("srhd,urd->srhu", q_rot, new_rope, preferred_element_type=jnp.float32)
    ) * scale
    causal = (jnp.arange(step_count)[:, None] >= jnp.arange(step_count)[None, :])[:, None, None, :]
    scores = jnp.where(causal, scores, -1e30)
    row_top = jnp.maximum(run_max, jnp.max(scores, axis=-1))
    factor = jnp.exp(run_max - row_top)
    weights = jnp.where(causal, jnp.exp(scores - row_top[..., None]), 0.0)
    total_sum = run_sum * factor + jnp.sum(weights, axis=-1)
    mixed_sum = run_out * factor[..., None] + jnp.einsum(
        "srhu,urd->srhd",
        weights.astype(jnp.bfloat16),
        new_latent,
        preferred_element_type=jnp.float32,
    )
    return mixed_sum / total_sum[..., None]


def local(
    q_latent, q_rope, cache_latent, cache_rope, new_latent, new_rope, lengths, selected, w_uv
):
    lat_all, rot_all = (
        lax.all_gather(q_latent, "ctx", axis=1, tiled=True),
        lax.all_gather(q_rope, "ctx", axis=1, tiled=True),
    )
    q_lat, q_rot = (
        lax.all_to_all(lat_all, "batch", split_axis=1, concat_axis=2, tiled=True),
        lax.all_to_all(rot_all, "batch", split_axis=1, concat_axis=2, tiled=True),
    )
    run_max, run_sum, run_out = local_partials(
        q_lat, q_rot, cache_latent, cache_rope, lengths, selected
    )
    run_max, run_sum, run_out = combined_all((run_max, run_sum, run_out), "ctx", combine)
    latent_out = finish(q_lat, q_rot, run_max, run_sum, run_out, new_latent, new_rope)
    value_weight = w_uv.astype(jnp.float32)
    return jnp.einsum(
        "srhd,hdv->srhv",
        lax.all_to_all(latent_out, "batch", split_axis=2, concat_axis=1, tiled=True),
        value_weight,
        precision=lax.Precision.HIGHEST,
    ).astype(jnp.bfloat16)


def solution(mesh):
    placed = (
        P(None, "ctx", "batch", None),
        P(None, "ctx", "batch", None),
        P("batch", "ctx", None),
        P("batch", "ctx", None),
        P(None, "batch", None),
        P(None, "batch", None),
        P("batch"),
        P(None, "batch", None, None),
        P("batch", None, None),
    )
    return jax.shard_map(
        local, mesh=mesh, in_specs=placed, out_specs=P(None, None, "batch", None), check_vma=False
    )
```

profile of v0, /device:TPU:1, one launch (start us, length us, event | category | flops | bytes accessed | tf_op | source)
XLA Modules:
  0.0 496.7 jit_solution(2999214996315492349)
XLA Ops:
  6.5 32.5 %all_gather.25 = bf16[4,32,4,64]{3,2,0,1:T(4,128)(2,1)S(1)} all-gather(bf16[4,1,4,64]{3,2,0,1:T(4,128)(2,1)} %bitcast.121), channel_id=1, replica_groups=mesh['batch'=16,'ctx'=32] {'ctx'}, dimensions={1}, use_global_device_ids=true | all-gather | bytes 67584 | tf_op jit(solution)/shard_map/all_gather | solution.py:133
  39.8 19.2 %all-to-all-start.1 = ((bf16[16,2,1024]{2,1,0:T(2,128)(2,1)}), bf16[16,2,1024]{2,1,0:T(2,128)(2,1)S(1)}, u32[]{:S(2)}, u32[]{:S(2)}) async-start(bf16[16,2,1024]{2,1,0:T(2,128)(2,1)} %reshape.62), calls=%async_computation.1 | async-start | bytes 131072 | tf_op jit(solution)/shard_map/all_to_all | solution.py:137
  59.0 40.5 %all_gather.24 = bf16[4,32,4,512]{3,2,0,1:T(4,128)(2,1)} all-gather(bf16[4,1,4,512]{3,2,0,1:T(4,128)(2,1)} %bitcast.118), channel_id=1, replica_groups=mesh['batch'=16,'ctx'=32] {'ctx'}, dimensions={1}, use_global_device_ids=true | all-gather | bytes 540672 | tf_op jit(solution)/shard_map/all_gather | solution.py:132
  99.6 19.0 %all-to-all-start = ((bf16[4,32,4,512]{3,2,0,1:T(4,128)(2,1)}), bf16[4,32,4,512]{3,2,0,1:T(4,128)(2,1)S(1)}, u32[]{:S(2)}, u32[]{:S(2)}) async-start(bf16[4,32,4,512]{3,2,0,1:T(4,128)(2,1)} %all_gather.24), calls=%async_computation | async-start | bytes 1048576 | tf_op jit(solution)/shard_map/all_to_all | solution.py:136
  118.8 17.1 %all-to-all-done = bf16[4,32,4,512]{3,2,0,1:T(4,128)(2,1)S(1)} async-done(((bf16[4,32,4,512]{3,2,0,1:T(4,128)(2,1)}), bf16[4,32,4,512]{3,2,0,1:T(4,128)(2,1)S(1)}, u32[]{:S(2)}, u32[]{:S(2)}) %all-to-all-start) | async-done | bytes 524320 | tf_op jit(solution)/shard_map/all_to_all | solution.py:136
  136.4 17.4 %while.38 = (s32[]{:T(128)}, f32[4,2,64]{2,0,1:T(4,128)S(1)}, f32[4,2,64]{2,0,1:T(4,128)S(1)}, f32[4,2,64,512]{3,2,0,1:T(8,128)S(1)}, s32[4,2,8,3]{2,1,3,0:T(2,1...) while((s32[]{:T(128)}, f32[4,2,64]{2,0,1:T(4,128)S(1)}, ...), condition=%wide.region_7.8_spmd, body=%wide.region_0.7_spmd.sunk | while | flops 287181088 | bytes 6190109 | solution.py:103
  137.7 6.0 %conditional.2 = ((f32[4,2,64]{2,0,1:T(4,128)S(1)}, f32[4,2,64]{2,0,1:T(4,128)S(1)}, f32[4,2,64,512]{3,2,0,1:T(8,128)S(1)})) conditional(s32[]{:T(128)} %convert_element_type.34, (f32[4,2,64]{2,0,1:T(4,128)S(1)}, f32[4,2,64]{2,0,1:T(4,128)S(1)}, f32[4,2,64,512]{3,2,0,1:T(8,128)S(1)}) %tuple.90, (s32[]{:T(128)}, f32[4,2,64]{2,0,1:T(4,128)S(1)}, ...), branch_computations={%region_2.2_spmd, %region_3.6_spmd} | conditional | flops 287180864 | bytes 6188417 | solution.py:101
  139.2 1.4 fusion.5
  142.2 1.4 fusion.3
  146.4 6.0 %conditional.2 = ((f32[4,2,64]{2,0,1:T(4,128)S(1)}, f32[4,2,64]{2,0,1:T(4,128)S(1)}, f32[4,2,64,512]{3,2,0,1:T(8,128)S(1)})) conditional(s32[]{:T(128)} %convert_element_type.34, (f32[4,2,64]{2,0,1:T(4,128)S(1)}, f32[4,2,64]{2,0,1:T(4,128)S(1)}, f32[4,2,64,512]{3,2,0,1:T(8,128)S(1)}) %tuple.90, (s32[]{:T(128)}, f32[4,2,64]{2,0,1:T(4,128)S(1)}, ...), branch_computations={%region_2.2_spmd, %region_3.6_spmd} | conditional | flops 287180864 | bytes 6188417 | solution.py:101
  147.9 1.4 fusion.5
  151.0 1.4 fusion.3
  155.0 43.9 %all-gather.1 = f32[128,2,64]{2,1,0:T(2,128)S(1)} all-gather(f32[4,2,64]{2,1,0:T(2,128)S(1)} %copy.49), channel_id=3, replica_groups=mesh['batch'=16,'ctx'=32] {'ctx'}, dimensions={0}, use_global_device_ids=true | all-gather | bytes 67584 | tf_op jit(solution)/shard_map/all_gather | solution.py:12
  198.9 32.0 %all-gather = f32[128,2,64]{2,1,0:T(2,128)S(1)} all-gather(f32[4,2,64]{2,1,0:T(2,128)S(1)} %copy.48), channel_id=2, replica_groups=mesh['batch'=16,'ctx'=32] {'ctx'}, dimensions={0}, use_global_device_ids=true | all-gather | bytes 67584 | tf_op jit(solution)/shard_map/all_gather | solution.py:12
  231.4 167.1 %all-gather.5.cloned.1.call-done = f32[128,2,64,512]{3,2,1,0:T(8,128)} async-done(((f32[4,2,64,512]{3,2,1,0:T(8,128)}), f32[128,2,64,512]{3,2,1,0:T(8,128)}) %all-gather.5.cloned.1.call-update) | async-done | bytes 33554448 | tf_op jit(solution)/shard_map/all_gather | solution.py:12
  399.8 49.1 %while.39 = (s32[]{:T(128)}, f32[4,2,64]{2,1,0:T(2,128)S(1)}, f32[4,2,64]{2,1,0:T(2,128)S(1)}, f32[4,2,64,512]{3,2,1,0:T(8,128)S(1)}, f32[32,4,2,64]{3,2,1,0:T(2...) while((s32[]{:T(128)}, f32[4,2,64]{2,1,0:T(2,128)S(1)}, ...), condition=%wide.region_9.10_spmd, body=%wide.region_8.9_spmd.sunk | while | flops 789509 | bytes 3166351 | solution.py:18
  399.9 1.5 fusion.63
  401.4 1.5 fusion.63
  403.0 1.5 fusion.63
  404.6 1.5 fusion.63
  406.2 1.5 fusion.63
  407.8 1.5 fusion.63
  409.4 1.5 fusion.63
  410.9 1.5 fusion.63
  412.5 1.5 fusion.63
  414.1 1.5 fusion.63
  415.7 1.5 fusion.63
  417.3 1.5 fusion.63
  418.9 1.5 fusion.63
  420.4 1.5 fusion.63
  422.0 1.5 fusion.63
  423.6 1.5 fusion.63
  425.2 1.5 fusion.63
  426.8 1.5 fusion.63
  428.4 1.5 fusion.63
  429.9 1.5 fusion.63
  431.5 1.5 fusion.63
  433.1 1.5 fusion.63
  434.7 1.5 fusion.63
  436.3 1.5 fusion.63
  437.9 1.5 fusion.63
  439.4 1.5 fusion.63
  441.0 1.5 fusion.63
  442.6 1.5 fusion.63
  444.2 1.5 fusion.63
  445.8 1.5 fusion.63
  447.4 1.5 fusion.63
  450.3 36.9 %all_to_all.54 = f32[4,2,64,512]{3,0,1,2:T(4,128)S(1)} all-to-all(f32[4,2,64,512]{3,0,1,2:T(4,128)S(1)} %copy.58), channel_id=1, replica_groups=mesh['batch'=16,'ctx'=32] {'batch'}, dimensions={2} | all-to-all | bytes 2097152 | tf_op jit(solution)/shard_map/all_to_all | solution.py:147
  (100 shorter events, 18.3 us)
Async XLA Ops:
  6.5 482.0 %copy-start = (bf16[4,512,128]{2,1,0:T(8,128)(2,1)S(1)}, bf16[4,512,128]{2,1,0:T(8,128)(2,1)}, u32[]{:S(2)}) copy-start(bf16[4,512,128]{2,1,0:T(8,128)(2,1)} %param.23) | copy-start | bytes 1572868
  39.8 59.7 %all-to-all-start.1 = ((bf16[16,2,1024]{2,1,0:T(2,128)(2,1)}), bf16[16,2,1024]{2,1,0:T(2,128)(2,1)S(1)}, u32[]{:S(2)}, u32[]{:S(2)}) async-start(bf16[16,2,1024]{2,1,0:T(2,128)(2,1)} %reshape.62), calls=%async_computation.1 | async-start | bytes 131072 | tf_op jit(solution)/shard_map/all_to_all | solution.py:137
  99.5 36.8 %copy-start.1 = (s32[4,2,8,3]{2,1,3,0:T(2,128)S(1)}, s32[4,2,8,3]{2,1,3,0:T(2,128)}, u32[]{:S(2)}) copy-start(s32[4,2,8,3]{2,1,3,0:T(2,128)} %param.22) | copy-start | bytes 2308
  99.5 36.8 %copy-start.4 = (s32[2]{0:T(128)S(1)}, s32[2]{0:T(128)}, u32[]{:S(2)}) copy-start(s32[2]{0:T(128)} %param.21) | copy-start | bytes 28
  99.6 36.3 %all-to-all-start = ((bf16[4,32,4,512]{3,2,0,1:T(4,128)(2,1)}), bf16[4,32,4,512]{3,2,0,1:T(4,128)(2,1)S(1)}, u32[]{:S(2)}, u32[]{:S(2)}) async-start(bf16[4,32,4,512]{3,2,0,1:T(4,128)(2,1)} %all_gather.24), calls=%async_computation | async-start | bytes 1048576 | tf_op jit(solution)/shard_map/all_to_all | solution.py:136
  118.6 279.9 %all-gather.5.cloned.1.call-start = ((), (), s32[]{:S(2)}) async-start(), calls=%async_computation.3 | async-start | bytes 34603008 | tf_op jit(solution)/shard_map/all_gather | solution.py:12
  153.8 77.0 %copy-start.2 = (bf16[4,2,512]{2,1,0:T(2,128)(2,1)S(1)}, bf16[4,2,512]{2,1,0:T(2,128)(2,1)}, u32[]{:S(2)}) copy-start(bf16[4,2,512]{2,1,0:T(2,128)(2,1)} %param.19) | copy-start | bytes 24580
  153.8 77.3 %copy-start.3 = (bf16[4,2,64]{2,1,0:T(2,128)(2,1)S(1)}, bf16[4,2,64]{2,1,0:T(2,128)(2,1)}, u32[]{:S(2)}) copy-start(bf16[4,2,64]{2,1,0:T(2,128)(2,1)} %param.20) | copy-start | bytes 3076
Sparse Core Ops, SparseCore 0:
  155.1 243.3 all-gather.4
where the time goes:
time: 499 us; the launch traced here: 497 us
  blocking collectives  186 us (37%)
  waiting for transfers between devices  184 us (37%)
  other arithmetic  52.9 us (11%)
  starting transfers between devices  38.3 us (8%)
  between operations  13.6 us (3%)
  matrix products  10 us (2%)
  local copies, waits for them, and re-layouts  8.21 us (2%)
    all_gather x1, waiting for transfers between devices, combined_all(): everything = jax.tree.map(lambda part: lax.all_gather(part, axis), value)  167 us
    all_gather x2, blocking collectives, combined_all(): everything = jax.tree.map(lambda part: lax.all_gather(part, axis), value)  75.8 us
    add x31, other arithmetic, combine(): first_out * first_factor[..., None] + second_out * second_factor[..., None]  47.3 us
    all_gather x1, blocking collectives, local(): lax.all_gather(q_latent, 'ctx', axis=1, tiled=True)  40.5 us
    all_to_all x1, blocking collectives, local(): lax.all_to_all(latent_out, 'batch', split_axis=2, concat_axis=1, tiled=True)  36.9 us
    all_gather x1, blocking collectives, local(): lax.all_gather(q_rope, 'ctx', axis=1, tiled=True)  32.5 us
    all_to_all x1, starting transfers between devices, local(): lax.all_to_all(rot_all, 'batch', split_axis=1, concat_axis=2, tiled=True)  19.2 us
    all_to_all x1, starting transfers between devices, local(): lax.all_to_all(lat_all, 'batch', split_axis=1, concat_axis=2, tiled=True)  19 us
  transfers between devices with their start and end apart: 3, of which 2 were waited for; matrix products, arithmetic and copies ran while one was open for 0% of the time, Pallas kernels for 0%

commit v1 on v0

v1 whole, which is shorter than its diff:
```python
import functools

import jax
import jax.numpy as jnp
from jax import lax
from jax.experimental import pallas as pl
from jax.experimental.pallas import tpu as pltpu
from jax.sharding import PartitionSpec as P

MESH = pl.DeviceIdType.MESH
KL = 512
KR = 64
VH = 128
BLOCK = 512
STEPS = 4
NX = 4
LOCAL_HEADS = 4
ROWS = STEPS * LOCAL_HEADS
WIDE = KL + 128
SCALE = (VH + KR) ** (-0.5)
NEG = -1e30
LAST = (((1,), (1,)), ((), ()))
FIRST = (((1,), (0,)), ((), ()))


def column(x, core):
    source_core = (x // 2 + core) % 2
    source_x = x + source_core * (NX - 1 - 2 * x)
    request = source_x % 2
    return request, source_core, source_x


def packed(out, top, total):
    lane = lax.broadcasted_iota(jnp.int32, (out.shape[0], 128), 1)
    high = total.astype(jnp.bfloat16).astype(jnp.float32)
    stats = jnp.where(lane == 0, top, jnp.where(lane == 1, high, jnp.where(lane == 2, total - high, 0.0)))
    return jnp.concatenate([out.astype(jnp.bfloat16), stats.astype(jnp.bfloat16)], axis=1)


def merged(parts, top):
    stats = [part[:, KL:].astype(jnp.float32) for part in parts]
    for stat in stats:
        top = stat[:, 0:1] if top is None else jnp.maximum(top, stat[:, 0:1])
    out, total = None, None
    for part, stat in zip(parts, stats):
        factor = jnp.exp(stat[:, 0:1] - top)
        share = factor * (stat[:, 1:2] + stat[:, 2:3])
        term = factor * part[:, :KL].astype(jnp.float32)
        out = term if out is None else out + term
        total = share if total is None else total + share
    return out, top, total


def kernel(
    n,
    length_ref, ql_ref, qr_ref, sel_ref, nl_ref, nr_ref, lat_hbm, rope_hbm, w_hbm,
    out_ref,
    lat, rope, w, rows32, mine, q_all, keep, part, part_in, joint, joint_in, done, done_in, gathered,
    local_sem, perm_sem, y_send, y_recv, x_send, x_recv, px_send, px_recv, py_send, py_recv,
    back_sem, oy_send, oy_recv, ox_send, ox_recv,
):
    b, c = lax.axis_index("batch"), lax.axis_index("ctx")
    z, core = b // 2, b % 2
    y, x = c // NX, c % NX
    half = n // 2

    loads = [
        pltpu.make_async_copy(src, dst, local_sem.at[k])
        for k, (src, dst) in enumerate(((lat_hbm, lat), (rope_hbm, rope), (w_hbm, w)))
    ]
    for load in loads:
        load.start()

    def at_y(step):
        return (b, ((y + step + n) % n) * NX + x)

    def at_x(step):
        return (b, y * NX + (x + step + NX) % NX)

    request, source_core, source_x = column(x, core)
    own = request * 2 + source_core
    origin = (((y + half) % n) * 2 + source_core, z * NX + source_x)
    goal_x = x + core * (NX - 1 - 2 * x)
    goal = (y * 2 + x // 2, ((z + half) % n) * NX + goal_x)
    goal_slot = (x % 2) * 2 + core

    barrier = pltpu.get_barrier_semaphore()

    @pl.loop(1, n)
    def _(d):
        pl.semaphore_signal(barrier, inc=1, device_id=at_y(d), device_id_type=MESH)

    @pl.loop(1, NX)
    def _(d):
        pl.semaphore_signal(barrier, inc=1, device_id=at_x(d), device_id_type=MESH)

    pl.semaphore_signal(barrier, inc=1, device_id=goal, device_id_type=MESH)
    pl.semaphore_signal(barrier, inc=1, device_id=origin, device_id_type=MESH)

    for t in range(STEPS):
        span = pl.ds(t * LOCAL_HEADS, LOCAL_HEADS)
        rows32[span, :KL] = ql_ref[t, 0].astype(jnp.float32)
        rows32[span, KL:KL + KR] = qr_ref[t, 0].astype(jnp.float32)
    rows32[:, KL + KR:] = jnp.zeros((ROWS, WIDE - KL - KR), jnp.float32)
    mine[...] = rows32[...].astype(jnp.bfloat16)

    pl.semaphore_wait(barrier, n - 1 + NX - 1 + 2)

    def remote(src, dst, send, recv, device):
        return pltpu.make_async_remote_copy(
            src_ref=src, dst_ref=dst, send_sem=send, recv_sem=recv, device_id=device, device_id_type=MESH
        )

    permute = remote(mine, q_all.at[goal_slot, (z + half) % n], perm_sem.at[0], perm_sem.at[1], goal)
    permute.start()

    tall = n * ROWS
    row = lax.broadcasted_iota(jnp.int32, (tall, STEPS * n), 0)
    unit = lax.broadcasted_iota(jnp.int32, (tall, STEPS * n), 1)
    group = (row // ROWS + half) % n
    step = (row % ROWS) // LOCAL_HEADS
    spread = jnp.where(unit == step * n + group, 1.0, 0.0).astype(jnp.bfloat16)
    lane = lax.broadcasted_iota(jnp.int32, (STEPS * n, 128), 1)
    for r in range(2):
        chosen = jnp.concatenate([sel_ref[t, r] for t in range(STEPS)], axis=0)
        hits = [
            jnp.max(jnp.where(chosen == c * 2 + k, 1.0, 0.0), axis=1, keepdims=True) for k in range(2)
        ]
        table = jnp.where(lane == 0, hits[0], jnp.where(lane == 1, hits[1], 0.0)).astype(jnp.bfloat16)
        keep[r] = lax.dot_general(spread, table, FIRST, preferred_element_type=jnp.float32)

    permute.wait_recv()

    def y_copy(d):
        slot = q_all.at[own, y]
        return remote(slot, slot, y_send.at[d - 1], y_recv.at[d - 1], at_y(d))

    def x_copy(d, e):
        slot = q_all.at[own, (y - e + n) % n]
        return remote(slot, slot, x_send.at[d - 1, e], x_recv.at[d - 1, e], at_x(d))

    @pl.loop(1, n)
    def _(s):
        y_copy(s % 2 * ((s + 1) // 2) + (1 - s % 2) * (n - s // 2)).start()

    for d in (1, 3, 2):
        x_copy(d, 0).start()

    q_own = q_all[own, y].astype(jnp.float32)
    row_step = lax.broadcasted_iota(jnp.int32, (ROWS, 1), 0) // LOCAL_HEADS
    second = request.astype(jnp.float32)
    new_rows, new_scores = [], []
    for u in range(STEPS):
        both = nl_ref[u].astype(jnp.float32)
        both_rope = nr_ref[u].astype(jnp.float32)
        new_row = both[0:1] * (1.0 - second) + both[1:2] * second
        new_rope = both_rope[0:1] * (1.0 - second) + both_rope[1:2] * second
        score = jnp.sum(q_own[:, :KL] * new_row, axis=1, keepdims=True)
        score = (score + jnp.sum(q_own[:, KL:KL + KR] * new_rope, axis=1, keepdims=True)) * SCALE
        new_rows.append(new_row)
        new_scores.append(jnp.where(row_step >= u, score, NEG))

    @pl.loop(1, n)
    def _(s):
        e = s % 2 * ((s + 1) // 2) + (1 - s % 2) * (n - s // 2)
        y_copy(e).wait_recv()
        for d in (1, 3, 2):
            x_copy(d, e).start()

    loads[0].wait()
    loads[1].wait()

    def px_copy(d):
        return remote(part.at[d], part_in.at[d - 1], px_send.at[d - 1], px_recv.at[d - 1], at_x(-d))

    @pl.loop(0, NX)
    def _(s):
        d = s + (s // 2) * (5 - 2 * s)
        r, from_core, _ = column((x - d + NX) % NX, core)

        @pl.when(d > 0)
        def _():
            @pl.loop(0, n)
            def _(e):
                x_copy(d, e).wait_recv()

        query = q_all[r * 2 + from_core].reshape(tall, WIDE)
        scores = lax.dot_general(query[:, :KL], lat[r], LAST, preferred_element_type=jnp.float32)
        scores = scores + lax.dot_general(
            query[:, KL:KL + KR], rope[r], LAST, preferred_element_type=jnp.float32
        )
        scores = scores * SCALE
        length = length_ref[r]
        hits = keep[r]
        place = lax.broadcasted_iota(jnp.int32, (tall, BLOCK), 1)
        masks, masked = [], []
        for k in range(2):
            mask = (hits[:, k:k + 1] > 0.5) & (place + (c * 2 + k) * BLOCK < length)
            masks.append(mask)
            masked.append(jnp.where(mask, scores[:, k * BLOCK:(k + 1) * BLOCK], NEG))
        top = jnp.maximum(
            jnp.max(masked[0], axis=1, keepdims=True), jnp.max(masked[1], axis=1, keepdims=True)
        )
        top = top.astype(jnp.bfloat16).astype(jnp.float32)
        weights = [jnp.where(m, jnp.exp(v - top), 0.0) for m, v in zip(masks, masked)]
        total = jnp.sum(weights[0], axis=1, keepdims=True) + jnp.sum(weights[1], axis=1, keepdims=True)
        rounded = jnp.concatenate([v.astype(jnp.bfloat16) for v in weights], axis=1)
        out = lax.dot_general(rounded, lat[r], FIRST, preferred_element_type=jnp.float32)
        part[d] = packed(out, top, total).reshape(n, ROWS, WIDE)

        @pl.when(d > 0)
        def _():
            px_copy(d).start()

    for d in (1, 3, 2):
        px_copy(d).wait_recv()
    parts = [part[0]] + [part_in[k] for k in range(NX - 1)]
    out, top, total = merged([v.reshape(tall, WIDE) for v in parts], None)
    joint[...] = packed(out, top, total).reshape(n, ROWS, WIDE)

    def py_copy(d):
        return remote(
            joint.at[(y + d) % n], joint_in.at[d - 1], py_send.at[d - 1], py_recv.at[d - 1], at_y(d)
        )

    @pl.loop(1, n)
    def _(s):
        py_copy(s % 2 * ((s + 1) // 2) + (1 - s % 2) * (n - s // 2)).start()

    @pl.loop(1, n)
    def _(d):
        py_copy(d).wait_recv()

    new_top = new_scores[0]
    for score in new_scores[1:]:
        new_top = jnp.maximum(new_top, score)
    out, top, total = merged([joint[y]] + [joint_in[k] for k in range(n - 1)], new_top)
    for u in range(STEPS):
        weight = jnp.where(row_step >= u, jnp.exp(new_scores[u] - top), 0.0)
        total = total + weight
        out = out + weight.astype(jnp.bfloat16).astype(jnp.float32) * new_rows[u]
    done[...] = out / total

    back = remote(done, done_in, back_sem.at[0], back_sem.at[1], origin)
    back.start()
    loads[2].wait()
    back.wait_recv()
    value = done_in[...]
    high = value.astype(jnp.bfloat16)
    rest = value - high.astype(jnp.float32)
    middle = rest.astype(jnp.bfloat16)
    low = (rest - middle.astype(jnp.float32)).astype(jnp.bfloat16)
    terms = jnp.concatenate([high, middle, low], axis=0)
    row_head = lax.broadcasted_iota(jnp.int32, (ROWS, VH), 0) % LOCAL_HEADS
    result = jnp.zeros((ROWS, VH), jnp.float32)
    for h in range(LOCAL_HEADS):
        product = lax.dot_general(terms, w[h], FIRST, preferred_element_type=jnp.float32)
        product = product[:ROWS] + (product[ROWS:2 * ROWS] + product[2 * ROWS:])
        result = jnp.where(row_head == h, product, result)
    gathered[x, y] = result.astype(jnp.bfloat16)

    def oy_copy(d):
        slot = gathered.at[x, y]
        return remote(slot, slot, oy_send.at[d - 1], oy_recv.at[d - 1], at_y(d))

    def ox_copy(d):
        slot = gathered.at[x]
        return remote(slot, slot, ox_send.at[d - 1], ox_recv.at[d - 1], at_x(d))

    @pl.loop(1, n)
    def _(s):
        oy_copy(s % 2 * ((s + 1) // 2) + (1 - s % 2) * (n - s // 2)).start()

    @pl.loop(1, n)
    def _(d):
        oy_copy(d).wait_recv()

    for d in (1, 3, 2):
        ox_copy(d).start()
    for d in (1, 3, 2):
        ox_copy(d).wait_recv()
    out_ref[...] = gathered[...]

    permute.wait_send()
    back.wait_send()

    @pl.loop(1, n)
    def _(d):
        y_copy(d).wait_send()
        py_copy(d).wait_send()
        oy_copy(d).wait_send()

    @pl.loop(1, NX)
    def _(d):
        px_copy(d).wait_send()
        ox_copy(d).wait_send()

        @pl.loop(0, n)
        def _(e):
            x_copy(d, e).wait_send()


def local(
    q_latent, q_rope, cache_latent, cache_rope, new_latent, new_rope, lengths, selected, w_uv
):
    n = lax.axis_size("ctx") // NX
    held = cache_latent.shape[1]
    bf16, f32 = jnp.bfloat16, jnp.float32
    dma = pltpu.SemaphoreType.DMA
    vmem, anywhere = pl.BlockSpec(memory_space=pltpu.VMEM), pl.BlockSpec(memory_space=pl.ANY)
    out = pl.pallas_call(
        functools.partial(kernel, n),
        out_shape=jax.ShapeDtypeStruct((NX, n, ROWS, VH), bf16),
        in_specs=[pl.BlockSpec(memory_space=pltpu.SMEM)] + [vmem] * 5 + [anywhere] * 3,
        out_specs=vmem,
        scratch_shapes=[
            pltpu.VMEM((2, held, KL), bf16),
            pltpu.VMEM((2, held, KR), bf16),
            pltpu.VMEM((LOCAL_HEADS, KL, VH), bf16),
            pltpu.VMEM((ROWS, WIDE), f32),
            pltpu.VMEM((ROWS, WIDE), bf16),
            pltpu.VMEM((NX, n, ROWS, WIDE), bf16),
            pltpu.VMEM((2, n * ROWS, 128), f32),
            pltpu.VMEM((NX, n, ROWS, WIDE), bf16),
            pltpu.VMEM((NX - 1, n, ROWS, WIDE), bf16),
            pltpu.VMEM((n, ROWS, WIDE), bf16),
            pltpu.VMEM((n - 1, ROWS, WIDE), bf16),
            pltpu.VMEM((ROWS, KL), f32),
            pltpu.VMEM((ROWS, KL), f32),
            pltpu.VMEM((NX, n, ROWS, VH), bf16),
            dma((3,)),
            dma((2,)),
            dma((n - 1,)), dma((n - 1,)),
            dma((NX - 1, n)), dma((NX - 1, n)),
            dma((NX - 1,)), dma((NX - 1,)),
            dma((n - 1,)), dma((n - 1,)),
            dma((2,)),
            dma((n - 1,)), dma((n - 1,)),
            dma((NX - 1,)), dma((NX - 1,)),
        ],
        compiler_params=pltpu.CompilerParams(
            collective_id=0, has_side_effects=True, vmem_limit_bytes=40 * 1024 * 1024
        ),
    )(lengths, q_latent, q_rope, selected, new_latent, new_rope, cache_latent, cache_rope, w_uv)
    out = out.reshape(NX, n, STEPS, LOCAL_HEADS, VH)
    return jnp.transpose(out, (2, 1, 0, 3, 4)).reshape(STEPS, NX * n, LOCAL_HEADS, VH)


def solution(mesh):
    placed = (
        P(None, "ctx", "batch", None),
        P(None, "ctx", "batch", None),
        P("batch", "ctx", None),
        P("batch", "ctx", None),
        P(None, "batch", None),
        P(None, "batch", None),
        P("batch"),
        P(None, "batch", None, None),
        P("batch", None, None),
    )
    return jax.shard_map(
        local, mesh=mesh, in_specs=placed, out_specs=P(None, None, "batch", None), check_vma=False
    )
```

time: 499 us -> 72.7 us (0.15)
  blocking collectives: 186 us -> 0 us
  waiting for transfers between devices: 184 us -> 0 us
  Pallas kernels: 0 us -> 63.5 us
  other arithmetic: 52.9 us -> 0 us
  starting transfers between devices: 38.3 us -> 0 us
  between operations: 13.6 us -> 0.03 us
  matrix products: 10 us -> 0 us
    all_gather x1 -> x0, waiting for transfers between devices: 167 us -> none  [combined_all(): everything = jax.tree.map(lambda part: lax.all_gather(part, axis), value)]
    all_gather x4 -> x0, blocking collectives: 149 us -> none  [the longest x2 75.8 us: combined_all(): everything = jax.tree.map(lambda part: lax.all_gather(part, axis), value)]
    pallas_call x0 -> x1, Pallas kernels: none -> 63.5 us  [local(): pl.pallas_call(functools.partial(kernel, n), out_shape=jax.ShapeDtypeStru...]
    add x63 -> x0, other arithmetic: 48.2 us -> none  [the longest x31 47.3 us: combine(): first_out * first_factor[..., None] + second_out * second_factor[..., None]]
    all_to_all x2 -> x0, starting transfers between devices: 38.2 us -> none  [the longest x1 19.2 us: local(): lax.all_to_all(rot_all, 'batch', split_axis=1, concat_axis=2, tiled=True)]
    all_to_all x1 -> x0, blocking collectives: 36.9 us -> none  [local(): lax.all_to_all(latent_out, 'batch', split_axis=2, concat_axis=1, tiled=True)]
    all_to_all x2 -> x0, waiting for transfers between devices: 17.1 us -> none  [the longest x1 17.1 us: local(): lax.all_to_all(lat_all, 'batch', split_axis=1, concat_axis=2, tiled=True)]
    dot_general x10 -> x0, matrix products: 10 us -> none  [the longest x2 2.9 us: attend(): jnp.einsum('shj,jd->shd', weights.astype(jnp.bfloat16), lat_rows, preferr...]
  transfers between devices with their start and end apart: 3 -> 0, of which waited for: 2 -> 0; matrix products, arithmetic and copies ran while one was open for 0% -> 0% of each run, Pallas kernels for 0% -> 0%
where the time goes in v1:
time: 72.7 us; the launch traced here: 72.3 us
  Pallas kernels  63.5 us (87%)
  local copies, waits for them, and re-layouts  8.81 us (12%)
    pallas_call x1, Pallas kernels, local(): pl.pallas_call(functools.partial(kernel, n), out_shape=jax.ShapeDtypeStru...  63.5 us
    unnamed x16, local copies, waits for them, and re-layouts  8.11 us

profile of v1, /device:TPU:1, one launch (start us, length us, event | category | flops | bytes accessed | tf_op | source)
XLA Modules:
  0.0 72.3 jit_solution(5558774343481653509)
XLA Ops:
  0.0 0.8 %copy.10.sel_ref = s32[4,2,8,3]{3,2,1,0:T(8,128)S(1)} copy(s32[4,2,8,3]{2,1,3,0:T(2,128)} %param.16) | data formatting | bytes 1536 | tf_op args[7]
  0.8 1.2 %copy.11.rope_hbm = bf16[2,1024,64]{2,1,0:T(8,128)(2,1)S(1)} copy(bf16[2,1024,64]{1,2,0:T(8,128)(2,1)} %param.12) | data formatting | bytes 524288 | tf_op args[3]
  2.0 0.0 copy-start
  2.1 1.6 %copy-done = bf16[2,1024,512]{2,1,0:T(8,128)(2,1)S(1)} copy-done((bf16[2,1024,512]{2,1,0:T(8,128)(2,1)S(1)}, bf16[2,1024,512]{2,1,0:T(8,128)(2,1)}, u32[]{:S(2)}) %copy-start) | copy-done | bytes 2097176
  3.6 0.0 copy-start.1
  3.6 1.0 %copy-done.1 = bf16[4,512,128]{2,1,0:T(8,128)(2,1)S(1)} copy-done((bf16[4,512,128]{2,1,0:T(8,128)(2,1)S(1)}, bf16[4,512,128]{2,1,0:T(8,128)(2,1)}, u32[]{:S(2)}) %copy-start.1) | copy-done | bytes 524312
  4.7 0.0 copy-start.2
  4.7 0.7 copy-done.2
  5.4 0.0 copy-start.3
  5.4 0.7 copy-done.3
  6.1 0.0 copy-start.4
  6.1 0.7 copy-done.4
  6.8 0.0 copy-start.5
  6.8 0.7 copy-done.5
  7.5 0.0 copy-start.6
  7.5 0.7 copy-done.6
  8.1 63.5 %shard_map.91 = bf16[4,8,16,128]{3,2,1,0:T(8,128)(2,1)S(1)} custom-call(s32[2]{0:T(128)S(1)} %copy-done.6, bf16[4,1,4,512]{3,2,1,0:T(4,128)(2,1)S(1)} %copy-done.2, bf16[4,1,4,64]{3,2,1,0:T(4,128)(2,1)S(1)} %copy-done.4, s32[4,2,8,3]{3,2,1,0:T(8,128)S(1)} %copy.10.sel_ref, bf16[4,2,512]{2,1,0:T(2,128)(2,1)S(1)} %copy-done.3, ...), custom_call_target="tpu_custom_call" | custom-call | tf_op jit(solution)/shard_map/pallas_call | solution.py:311
  71.6 0.7 copy.12
Async XLA Ops:
  2.0 1.6 %copy-start = (bf16[2,1024,512]{2,1,0:T(8,128)(2,1)S(1)}, bf16[2,1024,512]{2,1,0:T(8,128)(2,1)}, u32[]{:S(2)}) copy-start(bf16[2,1024,512]{2,1,0:T(8,128)(2,1)} %lat_hbm.1) | copy-start | bytes 6291460
  3.6 1.0 %copy-start.1 = (bf16[4,512,128]{2,1,0:T(8,128)(2,1)S(1)}, bf16[4,512,128]{2,1,0:T(8,128)(2,1)}, u32[]{:S(2)}) copy-start(bf16[4,512,128]{2,1,0:T(8,128)(2,1)} %w_hbm.1) | copy-start | bytes 1572868
  4.7 0.7 copy-start.2
  5.4 0.7 copy-start.3
  6.1 0.7 copy-start.4
  6.8 0.7 copy-start.5
  7.5 0.7 copy-start.6

commit v2 on v1

--- a/solution.py
+++ b/solution.py
@@ -53,9 +53,9 @@
 
 def kernel(
     n,
-    length_ref, ql_ref, qr_ref, sel_ref, nl_ref, nr_ref, lat_hbm, rope_hbm, w_hbm,
+    length_hbm, ql_hbm, qr_hbm, sel_hbm, nl_hbm, nr_hbm, lat_hbm, rope_hbm, w_hbm,
     out_ref,
-    lat, rope, w, rows32, mine, q_all, keep, part, part_in, joint, joint_in, done, done_in, gathered,
+    length_ref, ql_ref, qr_ref, sel_ref, nl_ref, nr_ref, lat, rope, w, rows32, mine, q_all, keep, part, part_in, joint, joint_in, done, done_in, gathered,
     local_sem, perm_sem, y_send, y_recv, x_send, x_recv, px_send, px_recv, py_send, py_recv,
     back_sem, oy_send, oy_recv, ox_send, ox_recv,
 ):
@@ -64,10 +64,11 @@
     y, x = c // NX, c % NX
     half = n // 2
 
-    loads = [
-        pltpu.make_async_copy(src, dst, local_sem.at[k])
-        for k, (src, dst) in enumerate(((lat_hbm, lat), (rope_hbm, rope), (w_hbm, w)))
-    ]
+    pairs = (
+        (ql_hbm, ql_ref), (qr_hbm, qr_ref), (sel_hbm, sel_ref), (nl_hbm, nl_ref), (nr_hbm, nr_ref),
+        (length_hbm, length_ref), (lat_hbm, lat), (rope_hbm, rope), (w_hbm, w),
+    )
+    loads = [pltpu.make_async_copy(src, dst, local_sem.at[k]) for k, (src, dst) in enumerate(pairs)]
     for load in loads:
         load.start()
 
@@ -97,6 +98,8 @@
     pl.semaphore_signal(barrier, inc=1, device_id=goal, device_id_type=MESH)
     pl.semaphore_signal(barrier, inc=1, device_id=origin, device_id_type=MESH)
 
+    loads[0].wait()
+    loads[1].wait()
     for t in range(STEPS):
         span = pl.ds(t * LOCAL_HEADS, LOCAL_HEADS)
         rows32[span, :KL] = ql_ref[t, 0].astype(jnp.float32)
@@ -115,19 +118,25 @@
     permute.start()
 
     tall = n * ROWS
-    row = lax.broadcasted_iota(jnp.int32, (tall, STEPS * n), 0)
-    unit = lax.broadcasted_iota(jnp.int32, (tall, STEPS * n), 1)
-    group = (row // ROWS + half) % n
-    step = (row % ROWS) // LOCAL_HEADS
-    spread = jnp.where(unit == step * n + group, 1.0, 0.0).astype(jnp.bfloat16)
-    lane = lax.broadcasted_iota(jnp.int32, (STEPS * n, 128), 1)
+    row = lax.broadcasted_iota(jnp.int32, (tall, n), 0)
+    group = lax.broadcasted_iota(jnp.int32, (tall, n), 1)
+    spread = jnp.where(group == (row // ROWS + half) % n, 1.0, 0.0).astype(jnp.bfloat16)
+    loads[2].wait()
+    hits = []
+    for t in range(STEPS):
+        chosen = sel_ref[t]
+        for k in range(2):
+            hits.append(jnp.max(jnp.where(chosen == c * 2 + k, 1.0, 0.0), axis=0))
+    table = jnp.concatenate(hits, axis=0).astype(jnp.bfloat16)
+    marks = lax.dot_general(spread, table, LAST, preferred_element_type=jnp.float32)
+    lane = lax.broadcasted_iota(jnp.int32, (tall, STEPS * 4), 1)
+    step = lax.broadcasted_iota(jnp.int32, (tall, STEPS * 4), 0) % ROWS // LOCAL_HEADS
+    marks = jnp.where(lane // 4 == step, marks, 0.0).astype(jnp.bfloat16)
+    source = lax.broadcasted_iota(jnp.int32, (STEPS * 4, 128), 0) % 4
+    target = lax.broadcasted_iota(jnp.int32, (STEPS * 4, 128), 1)
     for r in range(2):
-        chosen = jnp.concatenate([sel_ref[t, r] for t in range(STEPS)], axis=0)
-        hits = [
-            jnp.max(jnp.where(chosen == c * 2 + k, 1.0, 0.0), axis=1, keepdims=True) for k in range(2)
-        ]
-        table = jnp.where(lane == 0, hits[0], jnp.where(lane == 1, hits[1], 0.0)).astype(jnp.bfloat16)
-        keep[r] = lax.dot_general(spread, table, FIRST, preferred_element_type=jnp.float32)
+        pick = jnp.where((target < 2) & (source == target * 2 + r), 1.0, 0.0).astype(jnp.bfloat16)
+        keep[r] = lax.dot_general(marks, pick, FIRST, preferred_element_type=jnp.float32)
 
     permute.wait_recv()
 
@@ -146,6 +155,8 @@
     for d in (1, 3, 2):
         x_copy(d, 0).start()
 
+    loads[3].wait()
+    loads[4].wait()
     q_own = q_all[own, y].astype(jnp.float32)
     row_step = lax.broadcasted_iota(jnp.int32, (ROWS, 1), 0) // LOCAL_HEADS
     second = request.astype(jnp.float32)
@@ -167,8 +178,8 @@
         for d in (1, 3, 2):
             x_copy(d, e).start()
 
-    loads[0].wait()
-    loads[1].wait()
+    for load in loads[5:8]:
+        load.wait()
 
     def px_copy(d):
         return remote(part.at[d], part_in.at[d - 1], px_send.at[d - 1], px_recv.at[d - 1], at_x(-d))
@@ -187,7 +198,7 @@
         query = q_all[r * 2 + from_core].reshape(tall, WIDE)
         scores = lax.dot_general(query[:, :KL], lat[r], LAST, preferred_element_type=jnp.float32)
         scores = scores + lax.dot_general(
-            query[:, KL:KL + KR], rope[r], LAST, preferred_element_type=jnp.float32
+            query[:, KL:KL + KR], rope[r], FIRST, preferred_element_type=jnp.float32
         )
         scores = scores * SCALE
         length = length_ref[r]
@@ -243,7 +254,7 @@
 
     back = remote(done, done_in, back_sem.at[0], back_sem.at[1], origin)
     back.start()
-    loads[2].wait()
+    loads[8].wait()
     back.wait_recv()
     value = done_in[...]
     high = value.astype(jnp.bfloat16)
@@ -304,18 +315,26 @@
     q_latent, q_rope, cache_latent, cache_rope, new_latent, new_rope, lengths, selected, w_uv
 ):
     n = lax.axis_size("ctx") // NX
+    selected = jnp.transpose(selected, (0, 3, 1, 2))
+    cache_rope = jnp.swapaxes(cache_rope, 1, 2)
     held = cache_latent.shape[1]
     bf16, f32 = jnp.bfloat16, jnp.float32
     dma = pltpu.SemaphoreType.DMA
-    vmem, anywhere = pl.BlockSpec(memory_space=pltpu.VMEM), pl.BlockSpec(memory_space=pl.ANY)
+    anywhere = pl.BlockSpec(memory_space=pl.ANY)
     out = pl.pallas_call(
         functools.partial(kernel, n),
         out_shape=jax.ShapeDtypeStruct((NX, n, ROWS, VH), bf16),
-        in_specs=[pl.BlockSpec(memory_space=pltpu.SMEM)] + [vmem] * 5 + [anywhere] * 3,
-        out_specs=vmem,
+        in_specs=[anywhere] * 9,
+        out_specs=pl.BlockSpec(memory_space=pltpu.VMEM),
         scratch_shapes=[
+            pltpu.SMEM((2,), jnp.int32),
+            pltpu.VMEM(q_latent.shape, bf16),
+            pltpu.VMEM(q_rope.shape, bf16),
+            pltpu.VMEM(selected.shape, jnp.int32),
+            pltpu.VMEM(new_latent.shape, bf16),
+            pltpu.VMEM(new_rope.shape, bf16),
             pltpu.VMEM((2, held, KL), bf16),
-            pltpu.VMEM((2, held, KR), bf16),
+            pltpu.VMEM((2, KR, held), bf16),
             pltpu.VMEM((LOCAL_HEADS, KL, VH), bf16),
             pltpu.VMEM((ROWS, WIDE), f32),
             pltpu.VMEM((ROWS, WIDE), bf16),
@@ -328,7 +347,7 @@
             pltpu.VMEM((ROWS, KL), f32),
             pltpu.VMEM((ROWS, KL), f32),
             pltpu.VMEM((NX, n, ROWS, VH), bf16),
-            dma((3,)),
+            dma((9,)),
             dma((2,)),
             dma((n - 1,)), dma((n - 1,)),
             dma((NX - 1, n)), dma((NX - 1, n)),
@@ -339,7 +358,7 @@
             dma((NX - 1,)), dma((NX - 1,)),
         ],
         compiler_params=pltpu.CompilerParams(
-            collective_id=0, has_side_effects=True, vmem_limit_bytes=40 * 1024 * 1024
+            collective_id=0, has_side_effects=True, vmem_limit_bytes=60 * 1024 * 1024
         ),
     )(lengths, q_latent, q_rope, selected, new_latent, new_rope, cache_latent, cache_rope, w_uv)
     out = out.reshape(NX, n, STEPS, LOCAL_HEADS, VH)

time: 72.7 us -> 65.5 us (0.901)
  local copies, waits for them, and re-layouts: 8.81 us -> 1.61 us
    unnamed x16 -> x0, local copies, waits for them, and re-layouts: 8.11 us -> none
    transpose x1, local copies, waits for them, and re-layouts: 0.7 us -> 1.61 us  [local(): jnp.transpose(out, (2, 1, 0, 3, 4)).reshape(STEPS, NX * n, LOCAL_HEADS, VH)]
where the time goes in v2:
time: 65.5 us; the launch traced here: 65.3 us
  Pallas kernels  63.7 us (97%)
  local copies, waits for them, and re-layouts  1.61 us (2%)
    pallas_call x1, Pallas kernels, local(): pl.pallas_call(functools.partial(kernel, n), out_shape=jax.ShapeDtypeStru...  63.7 us
    transpose x1, local copies, waits for them, and re-layouts, local(): jnp.transpose(out, (2, 1, 0, 3, 4)).reshape(STEPS, NX * n, LOCAL_HEADS, VH)  1.61 us

profile of v2, /device:TPU:1, one launch (start us, length us, event | category | flops | bytes accessed | tf_op | source)
XLA Modules:
  0.0 65.3 jit_solution(9117924006637352715)
XLA Ops:
  0.0 63.7 %shard_map.91 = bf16[4,8,16,128]{3,2,1,0:T(8,128)(2,1)} custom-call(s32[2]{0:T(128)} %length_hbm.1, bf16[4,1,4,512]{3,2,1,0:T(4,128)(2,1)} %ql_hbm.1, bf16[4,1,4,64]{3,2,1,0:T(4,128)(2,1)} %qr_hbm.1, s32[4,3,2,8]{3,2,1,0:T(2,128)} %bitcast.8, bf16[4,2,512]{2,1,0:T(2,128)(2,1)} %nl_hbm.1, bf16[4,2,64]{2,1,0:T(2,128)(2,1)} %nr_hbm.1, ...), custom_call_target="tpu_custom_call" | custom-call | tf_op jit(solution)/shard_map/pallas_call | solution.py:324
  63.7 1.6 %copy.10 = bf16[4,8,4,4,128]{4,3,2,1,0:T(4,128)(2,1)} copy(bf16[4,8,4,4,128]{4,3,0,1,2:T(4,128)(2,1)} %bitcast.6) | data formatting | bytes 262144 | tf_op jit(solution)/shard_map/transpose | solution.py:365

commit v3 on v2

v3 whole, which is shorter than its diff:
```python
import functools

import jax
import jax.numpy as jnp
from jax import lax
from jax.experimental import pallas as pl
from jax.experimental.pallas import tpu as pltpu
from jax.sharding import PartitionSpec as P

MESH = pl.DeviceIdType.MESH
KL = 512
KR = 64
VH = 128
BLOCK = 512
STEPS = 4
NX = 4
LOCAL_HEADS = 4
ROWS = STEPS * LOCAL_HEADS
WIDE = KL + 128
SCALE = (VH + KR) ** (-0.5)
NEG = -1e30
LAST = (((1,), (1,)), ((), ()))
FIRST = (((1,), (0,)), ((), ()))


def column(x, core):
    source_core = (x // 2 + core) % 2
    source_x = x + source_core * (NX - 1 - 2 * x)
    request = source_x % 2
    return request, source_core, source_x


def packed(out, top, total):
    lane = lax.broadcasted_iota(jnp.int32, (out.shape[0], 128), 1)
    high = total.astype(jnp.bfloat16).astype(jnp.float32)
    stats = jnp.where(lane == 0, top, jnp.where(lane == 1, high, jnp.where(lane == 2, total - high, 0.0)))
    return jnp.concatenate([out.astype(jnp.bfloat16), stats.astype(jnp.bfloat16)], axis=1)


def merged(parts, top):
    stats = [part[:, KL:].astype(jnp.float32)[:, :3] for part in parts]
    return joined([part[:, :KL] for part in parts], stats, top)


def joined(values, stats, top):
    for stat in stats:
        top = stat[:, 0:1] if top is None else jnp.maximum(top, stat[:, 0:1])
    out, total = None, None
    for value, stat in zip(values, stats):
        factor = jnp.exp(stat[:, 0:1] - top)
        share = factor * (stat[:, 1:2] + stat[:, 2:3])
        term = factor * value.astype(jnp.float32)
        out = term if out is None else out + term
        total = share if total is None else total + share
    return out, top, total


def kernel(
    n,
    length_hbm, ql_hbm, qr_hbm, sel_hbm, nl_hbm, nr_hbm, lat_hbm, rope_hbm, w_hbm,
    out_ref,
    length_ref, ql_ref, qr_ref, sel_ref, nl_ref, nr_ref, lat, rope, w, rows32, mine, q_all, keep,
    part, part_in, joint, joint_in, done, done_in, gathered,
    local_sem, q_send, q_recv, x_send, x_recv, px_send, px_recv, py_send, py_recv, back_sem,
    oy_send, oy_recv, ox_send, ox_recv,
):
    b, c = lax.axis_index("batch"), lax.axis_index("ctx")
    z, core = b // 2, b % 2
    y, x = c // NX, c % NX
    far = n // 2

    pairs = (
        (ql_hbm, ql_ref), (qr_hbm, qr_ref), (sel_hbm, sel_ref), (nl_hbm, nl_ref), (nr_hbm, nr_ref),
        (length_hbm, length_ref), (lat_hbm, lat), (rope_hbm, rope), (w_hbm, w),
    )
    loads = [pltpu.make_async_copy(src, dst, local_sem.at[k]) for k, (src, dst) in enumerate(pairs)]
    for load in loads:
        load.start()

    def at_y(step):
        return (b, ((y + step + n) % n) * NX + x)

    def at_x(step):
        return (b, y * NX + (x + step + NX) % NX)

    request, source_core, source_x = column(x, core)
    own = request * 2 + source_core
    goal_x = x + core * (NX - 1 - 2 * x)
    goal_column = (x % 2) * 2 + core
    itself = (y == z) & (x // 2 == core) & (goal_x == x)
    other = jnp.logical_not(itself)

    def goal(step):
        return (y * 2 + x // 2, ((y + step) % n) * NX + goal_x)

    def origin(step):
        return (((z + step) % n) * 2 + source_core, z * NX + source_x)

    barrier = pltpu.get_barrier_semaphore()

    def greet(device):
        pl.semaphore_signal(barrier, inc=1, device_id=device, device_id_type=MESH)

    @pl.loop(1, n)
    def _(d):
        greet(goal(d))
        greet(origin(d))
        greet(at_y(d))

    @pl.loop(1, NX)
    def _(d):
        greet(at_x(d))

    @pl.when(other)
    def _():
        greet(goal(0))
        greet(origin(0))

    loads[0].wait()
    loads[1].wait()
    for t in range(STEPS):
        span = pl.ds(t * LOCAL_HEADS, LOCAL_HEADS)
        rows32[span, :KL] = ql_ref[t, 0].astype(jnp.float32)
        rows32[span, KL:KL + KR] = qr_ref[t, 0].astype(jnp.float32)
    rows32[:, KL + KR:] = jnp.zeros((ROWS, WIDE - KL - KR), jnp.float32)
    mine[...] = rows32[...].astype(jnp.bfloat16)

    pl.semaphore_wait(barrier, 3 * (n - 1) + NX - 1 + 2 * other.astype(jnp.int32))

    def remote(src, dst, send, recv, device):
        return pltpu.make_async_remote_copy(
            src_ref=src, dst_ref=dst, send_sem=send, recv_sem=recv, device_id=device, device_id_type=MESH
        )

    def nearest(s):
        return s % 2 * ((s + 1) // 2) + (1 - s % 2) * ((n - s // 2) % n)

    def q_copy(d):
        return remote(mine, q_all.at[goal_column, z], q_send.at[d], q_recv.at[z], goal(d))

    def q_wait(k):
        slot = q_all.at[own, k]
        remote(slot, slot, q_send.at[0], q_recv.at[k], goal(0)).wait_recv()

    @pl.loop(1, n)
    def _(s):
        q_copy(nearest(n - s)).start()

    @pl.when(other)
    def _():
        q_copy(0).start()

    @pl.when(itself)
    def _():
        q_all[own, z] = mine[...]

    tall = n * ROWS
    row = lax.broadcasted_iota(jnp.int32, (tall, n), 0)
    group = lax.broadcasted_iota(jnp.int32, (tall, n), 1)
    spread = jnp.where(group == row // ROWS, 1.0, 0.0).astype(jnp.bfloat16)
    loads[2].wait()
    hits = []
    for t in range(STEPS):
        chosen = sel_ref[t]
        for k in range(2):
            hits.append(jnp.max(jnp.where(chosen == c * 2 + k, 1.0, 0.0), axis=0))
    table = jnp.concatenate(hits, axis=0).astype(jnp.bfloat16)
    marks = lax.dot_general(spread, table, LAST, preferred_element_type=jnp.float32)
    lane = lax.broadcasted_iota(jnp.int32, (tall, STEPS * 4), 1)
    step = lax.broadcasted_iota(jnp.int32, (tall, STEPS * 4), 0) % ROWS // LOCAL_HEADS
    marks = jnp.where(lane // 4 == step, marks, 0.0).astype(jnp.bfloat16)
    source = lax.broadcasted_iota(jnp.int32, (STEPS * 4, 128), 0) % 4
    target = lax.broadcasted_iota(jnp.int32, (STEPS * 4, 128), 1)
    for r in range(2):
        pick = jnp.where((target < 2) & (source == target * 2 + r), 1.0, 0.0).astype(jnp.bfloat16)
        kept = lax.dot_general(marks, pick, FIRST, preferred_element_type=jnp.float32)
        keep[r] = kept.reshape(n, ROWS, 128)

    def x_copy(d, k):
        slot = q_all.at[own, k]
        return remote(slot, slot, x_send.at[d - 1, k], x_recv.at[d - 1, k], at_x(d))

    @pl.loop(0, n)
    def _(k):

        @pl.when((k != z) | other)
        def _():
            q_wait(k)

        for d in (1, 3, 2):
            x_copy(d, k).start()

    for load in loads[3:8]:
        load.wait()

    def px_copy(d, half):
        target = column((x - d + NX) % NX, core)
        return remote(
            part.at[half, target[0] * 2 + target[1]], part_in.at[half, d - 1],
            px_send.at[d - 1, half], px_recv.at[d - 1, half], at_x(-d),
        )

    rows = 2 * far * ROWS
    lane = lax.broadcasted_iota(jnp.int32, (ROWS, 128), 1)

    @pl.loop(0, 4)
    def _(turn):
        half = turn // 2
        r = (request + 1 + turn) % 2
        request_x = 2 * core + r
        away = [(x - request_x - k * (NX - 1 - 2 * request_x) + 2 * NX) % NX for k in range(2)]
        for d in away:
            @pl.when(d > 0)
            def _():
                @pl.loop(half * far, half * far + far)
                def _(k):
                    x_copy(d, k).wait_recv()

        span = pl.ds(half * far, far)
        query = q_all[pl.ds(r * 2, 2), span].reshape(rows, WIDE)
        scores = lax.dot_general(query[:, :KL], lat[r], LAST, preferred_element_type=jnp.float32)
        scores = scores + lax.dot_general(
            query[:, KL:KL + KR], rope[r], FIRST, preferred_element_type=jnp.float32
        )
        scores = scores * SCALE
        length = length_ref[r]
        hits = keep[r, span].reshape(rows // 2, 128)
        hits = jnp.concatenate([hits, hits], axis=0)
        place = lax.broadcasted_iota(jnp.int32, (rows, BLOCK), 1)
        masks, masked = [], []
        for k in range(2):
            mask = (hits[:, k:k + 1] > 0.5) & (place + (c * 2 + k) * BLOCK < length)
            masks.append(mask)
            masked.append(jnp.where(mask, scores[:, k * BLOCK:(k + 1) * BLOCK], NEG))
        top = jnp.maximum(
            jnp.max(masked[0], axis=1, keepdims=True), jnp.max(masked[1], axis=1, keepdims=True)
        )
        top = top.astype(jnp.bfloat16).astype(jnp.float32)
        weights = [jnp.where(m, jnp.exp(v - top), 0.0) for m, v in zip(masks, masked)]
        total = jnp.sum(weights[0], axis=1, keepdims=True) + jnp.sum(weights[1], axis=1, keepdims=True)
        rounded = jnp.concatenate([v.astype(jnp.bfloat16) for v in weights], axis=1)
        out = lax.dot_general(rounded, lat[r], FIRST, preferred_element_type=jnp.float32)
        out = out.astype(jnp.bfloat16)
        high = total.astype(jnp.bfloat16).astype(jnp.float32)
        low = total - high
        for k in range(2):
            stats = jnp.zeros((ROWS, 128), jnp.float32)
            for j in range(far):
                at = slice((k * far + j) * ROWS, (k * far + j + 1) * ROWS)
                part[half, r * 2 + k, :, j * KL:(j + 1) * KL] = out[at]
                for m, term in enumerate((top, high, low)):
                    stats = jnp.where(lane == 3 * j + m, term[at], stats)
            part[half, r * 2 + k, :, far * KL:] = stats.astype(jnp.bfloat16)
        for d in away:
            @pl.when(d > 0)
            def _():
                px_copy(d, half).start()

    mine_k = (y + far) % n
    q_own = q_all[own, mine_k].astype(jnp.float32)
    row_step = lax.broadcasted_iota(jnp.int32, (ROWS, 1), 0) // LOCAL_HEADS
    second = request.astype(jnp.float32)
    new_rows, new_scores = [], []
    for u in range(STEPS):
        both = nl_ref[u].astype(jnp.float32)
        both_rope = nr_ref[u].astype(jnp.float32)
        new_row = both[0:1] * (1.0 - second) + both[1:2] * second
        new_rope = both_rope[0:1] * (1.0 - second) + both_rope[1:2] * second
        score = jnp.sum(q_own[:, :KL] * new_row, axis=1, keepdims=True)
        score = (score + jnp.sum(q_own[:, KL:KL + KR] * new_rope, axis=1, keepdims=True)) * SCALE
        new_rows.append(new_row)
        new_scores.append(jnp.where(row_step >= u, score, NEG))
    new_top = new_scores[0]
    for score in new_scores[1:]:
        new_top = jnp.maximum(new_top, score)

    def py_copy(k):
        to = (k + far) % n
        return remote(joint.at[k], joint_in.at[y], py_send.at[k], py_recv.at[y], (b, to * NX + x))

    @pl.loop(0, 2)
    def _(half):
        for d in (1, 3, 2):
            px_copy(d, half).wait_recv()
        stats = [part[half, own, :, far * KL:].astype(jnp.float32)]
        stats += [part_in[half, e, :, far * KL:].astype(jnp.float32) for e in range(NX - 1)]
        for j in range(far):
            at = slice(j * KL, (j + 1) * KL)
            values = [part[half, own, :, at]] + [part_in[half, e, :, at] for e in range(NX - 1)]
            three = [stat[:, 3 * j:3 * j + 3] for stat in stats]
            k = half * far + j
            joint[k] = packed(*joined(values, three, None))

            @pl.when(k != mine_k)
            def _():
                py_copy(k).start()

    joint_in[y] = joint[mine_k]

    @pl.loop(1, n)
    def _(d):
        k = (y + d) % n
        remote(joint.at[0], joint_in.at[k], py_send.at[0], py_recv.at[k], at_y(d)).wait_recv()

    out, top, total = merged([joint_in[k] for k in range(n)], new_top)
    for u in range(STEPS):
        weight = jnp.where(row_step >= u, jnp.exp(new_scores[u] - top), 0.0)
        total = total + weight
        out = out + weight.astype(jnp.bfloat16).astype(jnp.float32) * new_rows[u]
    done[...] = out / total

    back = remote(done, done_in, back_sem.at[0], back_sem.at[1], origin((mine_k - z + n) % n))
    back.start()
    loads[8].wait()
    back.wait_recv()
    value = done_in[...]

    high = value.astype(jnp.bfloat16)
    rest = value - high.astype(jnp.float32)
    middle = rest.astype(jnp.bfloat16)
    low = (rest - middle.astype(jnp.float32)).astype(jnp.bfloat16)
    terms = jnp.concatenate([high, middle, low], axis=0)
    row_head = lax.broadcasted_iota(jnp.int32, (ROWS, VH), 0) % LOCAL_HEADS
    result = jnp.zeros((ROWS, VH), jnp.float32)
    for h in range(LOCAL_HEADS):
        product = lax.dot_general(terms, w[h], FIRST, preferred_element_type=jnp.float32)
        product = product[:ROWS] + (product[ROWS:2 * ROWS] + product[2 * ROWS:])
        result = jnp.where(row_head == h, product, result)
    gathered[x, y] = result.astype(jnp.bfloat16)

    def oy_copy(d):
        slot = gathered.at[x, y]
        return remote(slot, slot, oy_send.at[d - 1], oy_recv.at[d - 1], at_y(d))

    def ox_copy(d):
        slot = gathered.at[x]
        return remote(slot, slot, ox_send.at[d - 1], ox_recv.at[d - 1], at_x(d))

    @pl.loop(1, n)
    def _(s):
        oy_copy(nearest(n - s)).start()

    @pl.loop(1, n)
    def _(d):
        oy_copy(d).wait_recv()

    for d in (2, 1, 3):
        ox_copy(d).start()
    for d in (1, 3, 2):
        ox_copy(d).wait_recv()
    out_ref[...] = gathered[...]

    back.wait_send()

    @pl.loop(1, n)
    def _(d):
        q_copy(d).wait_send()
        py_copy((mine_k + d) % n).wait_send()
        oy_copy(d).wait_send()

    @pl.when(other)
    def _():
        q_copy(0).wait_send()

    @pl.loop(1, NX)
    def _(d):
        px_copy(d, 0).wait_send()
        px_copy(d, 1).wait_send()
        ox_copy(d).wait_send()

        @pl.loop(0, n)
        def _(k):
            x_copy(d, k).wait_send()


def local(
    q_latent, q_rope, cache_latent, cache_rope, new_latent, new_rope, lengths, selected, w_uv
):
    n = lax.axis_size("ctx") // NX
    selected = jnp.transpose(selected, (0, 3, 1, 2))
    cache_rope = jnp.swapaxes(cache_rope, 1, 2)
    held = cache_latent.shape[1]
    bf16, f32 = jnp.bfloat16, jnp.float32
    dma = pltpu.SemaphoreType.DMA
    anywhere = pl.BlockSpec(memory_space=pl.ANY)
    out = pl.pallas_call(
        functools.partial(kernel, n),
        out_shape=jax.ShapeDtypeStruct((NX, n, ROWS, VH), bf16),
        in_specs=[anywhere] * 9,
        out_specs=pl.BlockSpec(memory_space=pltpu.VMEM),
        scratch_shapes=[
            pltpu.SMEM((2,), jnp.int32),
            pltpu.VMEM(q_latent.shape, bf16),
            pltpu.VMEM(q_rope.shape, bf16),
            pltpu.VMEM(selected.shape, jnp.int32),
            pltpu.VMEM(new_latent.shape, bf16),
            pltpu.VMEM(new_rope.shape, bf16),
            pltpu.VMEM((2, held, KL), bf16),
            pltpu.VMEM((2, KR, held), bf16),
            pltpu.VMEM((LOCAL_HEADS, KL, VH), bf16),
            pltpu.VMEM((ROWS, WIDE), f32),
            pltpu.VMEM((ROWS, WIDE), bf16),
            pltpu.VMEM((NX, n, ROWS, WIDE), bf16),
            pltpu.VMEM((2, n, ROWS, 128), f32),
            pltpu.VMEM((2, NX, ROWS, n // 2 * KL + 128), bf16),
            pltpu.VMEM((2, NX - 1, ROWS, n // 2 * KL + 128), bf16),
            pltpu.VMEM((n, ROWS, WIDE), bf16),
            pltpu.VMEM((n, ROWS, WIDE), bf16),
            pltpu.VMEM((ROWS, KL), f32),
            pltpu.VMEM((ROWS, KL), f32),
            pltpu.VMEM((NX, n, ROWS, VH), bf16),
            dma((9,)),
            dma((n,)), dma((n,)),
            dma((NX - 1, n)), dma((NX - 1, n)),
            dma((NX - 1, 2)), dma((NX - 1, 2)),
            dma((n,)), dma((n,)),
            dma((2,)),
            dma((n - 1,)), dma((n - 1,)),
            dma((NX - 1,)), dma((NX - 1,)),
        ],
        compiler_params=pltpu.CompilerParams(
            collective_id=0, has_side_effects=True, vmem_limit_bytes=60 * 1024 * 1024
        ),
    )(lengths, q_latent, q_rope, selected, new_latent, new_rope, cache_latent, cache_rope, w_uv)
    out = out.reshape(NX, n, STEPS, LOCAL_HEADS, VH)
    return jnp.transpose(out, (2, 1, 0, 3, 4)).reshape(STEPS, NX * n, LOCAL_HEADS, VH)


def solution(mesh):
    placed = (
        P(None, "ctx", "batch", None),
        P(None, "ctx", "batch", None),
        P("batch", "ctx", None),
        P("batch", "ctx", None),
        P(None, "batch", None),
        P(None, "batch", None),
        P("batch"),
        P(None, "batch", None, None),
        P("batch", None, None),
    )
    return jax.shard_map(
        local, mesh=mesh, in_specs=placed, out_specs=P(None, None, "batch", None), check_vma=False
    )
```

time: 65.5 us -> 59.3 us (0.905)
  Pallas kernels: 63.7 us -> 57.3 us
    pallas_call x1, Pallas kernels: 63.7 us -> 57.3 us  [local(): pl.pallas_call(functools.partial(kernel, n), out_shape=jax.ShapeDtypeStru...]
where the time goes in v3:
time: 59.3 us; the launch traced here: 59 us
  Pallas kernels  57.3 us (97%)
  local copies, waits for them, and re-layouts  1.61 us (3%)
    pallas_call x1, Pallas kernels, local(): pl.pallas_call(functools.partial(kernel, n), out_shape=jax.ShapeDtypeStru...  57.3 us
    transpose x1, local copies, waits for them, and re-layouts, local(): jnp.transpose(out, (2, 1, 0, 3, 4)).reshape(STEPS, NX * n, LOCAL_HEADS, VH)  1.61 us

profile of v3, /device:TPU:1, one launch (start us, length us, event | category | flops | bytes accessed | tf_op | source)
XLA Modules:
  0.0 59.0 jit_solution(3179926685194974496)
XLA Ops:
  0.0 57.3 %shard_map.91 = bf16[4,8,16,128]{3,2,1,0:T(8,128)(2,1)} custom-call(s32[2]{0:T(128)} %length_hbm.1, bf16[4,1,4,512]{3,2,1,0:T(4,128)(2,1)} %ql_hbm.1, bf16[4,1,4,64]{3,2,1,0:T(4,128)(2,1)} %qr_hbm.1, s32[4,3,2,8]{3,2,1,0:T(2,128)} %bitcast.8, bf16[4,2,512]{2,1,0:T(2,128)(2,1)} %nl_hbm.1, bf16[4,2,64]{2,1,0:T(2,128)(2,1)} %nr_hbm.1, ...), custom_call_target="tpu_custom_call" | custom-call | tf_op jit(solution)/shard_map/pallas_call | solution.py:386
  57.4 1.6 %copy.10 = bf16[4,8,4,4,128]{4,3,2,1,0:T(4,128)(2,1)} copy(bf16[4,8,4,4,128]{4,3,0,1,2:T(4,128)(2,1)} %bitcast.6) | data formatting | bytes 262144 | tf_op jit(solution)/shard_map/transpose | solution.py:426

commit v4 on v3

--- a/solution.py
+++ b/solution.py
@@ -68,6 +68,8 @@
     z, core = b // 2, b % 2
     y, x = c // NX, c % NX
     far = n // 2
+    few = max(1, n // 4)
+    groups = n // few
 
     pairs = (
         (ql_hbm, ql_ref), (qr_hbm, qr_ref), (sel_hbm, sel_ref), (nl_hbm, nl_ref), (nr_hbm, nr_ref),
@@ -200,10 +202,10 @@
             px_send.at[d - 1, half], px_recv.at[d - 1, half], at_x(-d),
         )
 
-    rows = 2 * far * ROWS
+    rows = 2 * few * ROWS
     lane = lax.broadcasted_iota(jnp.int32, (ROWS, 128), 1)
 
-    @pl.loop(0, 4)
+    @pl.loop(0, 2 * groups)
     def _(turn):
         half = turn // 2
         r = (request + 1 + turn) % 2
@@ -212,11 +214,11 @@
         for d in away:
             @pl.when(d > 0)
             def _():
-                @pl.loop(half * far, half * far + far)
+                @pl.loop(half * few, half * few + few)
                 def _(k):
                     x_copy(d, k).wait_recv()
 
-        span = pl.ds(half * far, far)
+        span = pl.ds(half * few, few)
         query = q_all[pl.ds(r * 2, 2), span].reshape(rows, WIDE)
         scores = lax.dot_general(query[:, :KL], lat[r], LAST, preferred_element_type=jnp.float32)
         scores = scores + lax.dot_general(
@@ -245,12 +247,12 @@
         low = total - high
         for k in range(2):
             stats = jnp.zeros((ROWS, 128), jnp.float32)
-            for j in range(far):
-                at = slice((k * far + j) * ROWS, (k * far + j + 1) * ROWS)
+            for j in range(few):
+                at = slice((k * few + j) * ROWS, (k * few + j + 1) * ROWS)
                 part[half, r * 2 + k, :, j * KL:(j + 1) * KL] = out[at]
                 for m, term in enumerate((top, high, low)):
                     stats = jnp.where(lane == 3 * j + m, term[at], stats)
-            part[half, r * 2 + k, :, far * KL:] = stats.astype(jnp.bfloat16)
+            part[half, r * 2 + k, :, few * KL:] = stats.astype(jnp.bfloat16)
         for d in away:
             @pl.when(d > 0)
             def _():
@@ -278,17 +280,17 @@
         to = (k + far) % n
         return remote(joint.at[k], joint_in.at[y], py_send.at[k], py_recv.at[y], (b, to * NX + x))
 
-    @pl.loop(0, 2)
+    @pl.loop(0, groups)
     def _(half):
         for d in (1, 3, 2):
             px_copy(d, half).wait_recv()
-        stats = [part[half, own, :, far * KL:].astype(jnp.float32)]
-        stats += [part_in[half, e, :, far * KL:].astype(jnp.float32) for e in range(NX - 1)]
-        for j in range(far):
+        stats = [part[half, own, :, few * KL:].astype(jnp.float32)]
+        stats += [part_in[half, e, :, few * KL:].astype(jnp.float32) for e in range(NX - 1)]
+        for j in range(few):
             at = slice(j * KL, (j + 1) * KL)
             values = [part[half, own, :, at]] + [part_in[half, e, :, at] for e in range(NX - 1)]
             three = [stat[:, 3 * j:3 * j + 3] for stat in stats]
-            k = half * far + j
+            k = half * few + j
             joint[k] = packed(*joined(values, three, None))
 
             @pl.when(k != mine_k)
@@ -333,8 +335,7 @@
         return remote(slot, slot, oy_send.at[d - 1], oy_recv.at[d - 1], at_y(d))
 
     def ox_copy(d):
-        slot = gathered.at[x]
-        return remote(slot, slot, ox_send.at[d - 1], ox_recv.at[d - 1], at_x(d))
+        return remote(gathered.at[x], out_ref.at[x], ox_send.at[d - 1], ox_recv.at[d - 1], at_x(d))
 
     @pl.loop(1, n)
     def _(s):
@@ -346,9 +347,11 @@
 
     for d in (2, 1, 3):
         ox_copy(d).start()
+    keep_own = pltpu.make_async_copy(gathered.at[x], out_ref.at[x], local_sem.at[9])
+    keep_own.start()
     for d in (1, 3, 2):
         ox_copy(d).wait_recv()
-    out_ref[...] = gathered[...]
+    keep_own.wait()
 
     back.wait_send()
 
@@ -364,8 +367,8 @@
 
     @pl.loop(1, NX)
     def _(d):
-        px_copy(d, 0).wait_send()
-        px_copy(d, 1).wait_send()
+        for half in range(groups):
+            px_copy(d, half).wait_send()
         ox_copy(d).wait_send()
 
         @pl.loop(0, n)
@@ -380,6 +383,7 @@
     selected = jnp.transpose(selected, (0, 3, 1, 2))
     cache_rope = jnp.swapaxes(cache_rope, 1, 2)
     held = cache_latent.shape[1]
+    few = max(1, n // 4)
     bf16, f32 = jnp.bfloat16, jnp.float32
     dma = pltpu.SemaphoreType.DMA
     anywhere = pl.BlockSpec(memory_space=pl.ANY)
@@ -387,7 +391,7 @@
         functools.partial(kernel, n),
         out_shape=jax.ShapeDtypeStruct((NX, n, ROWS, VH), bf16),
         in_specs=[anywhere] * 9,
-        out_specs=pl.BlockSpec(memory_space=pltpu.VMEM),
+        out_specs=anywhere,
         scratch_shapes=[
             pltpu.SMEM((2,), jnp.int32),
             pltpu.VMEM(q_latent.shape, bf16),
@@ -402,17 +406,17 @@
             pltpu.VMEM((ROWS, WIDE), bf16),
             pltpu.VMEM((NX, n, ROWS, WIDE), bf16),
             pltpu.VMEM((2, n, ROWS, 128), f32),
-            pltpu.VMEM((2, NX, ROWS, n // 2 * KL + 128), bf16),
-            pltpu.VMEM((2, NX - 1, ROWS, n // 2 * KL + 128), bf16),
+            pltpu.VMEM((n // few, NX, ROWS, few * KL + 128), bf16),
+            pltpu.VMEM((n // few, NX - 1, ROWS, few * KL + 128), bf16),
             pltpu.VMEM((n, ROWS, WIDE), bf16),
             pltpu.VMEM((n, ROWS, WIDE), bf16),
             pltpu.VMEM((ROWS, KL), f32),
             pltpu.VMEM((ROWS, KL), f32),
             pltpu.VMEM((NX, n, ROWS, VH), bf16),
-            dma((9,)),
+            dma((10,)),
             dma((n,)), dma((n,)),
             dma((NX - 1, n)), dma((NX - 1, n)),
-            dma((NX - 1, 2)), dma((NX - 1, 2)),
+            dma((NX - 1, n // few)), dma((NX - 1, n // few)),
             dma((n,)), dma((n,)),
             dma((2,)),
             dma((n - 1,)), dma((n - 1,)),

time: 59.3 us -> 56.8 us (0.958)
  Pallas kernels: 57.3 us -> 54.7 us
    pallas_call x1, Pallas kernels: 57.3 us -> 54.7 us  [local(): pl.pallas_call(functools.partial(kernel, n), out_shape=jax.ShapeDtypeStru...]
where the time goes in v4:
time: 56.8 us; the launch traced here: 56.3 us
  Pallas kernels  54.7 us (96%)
  local copies, waits for them, and re-layouts  1.61 us (3%)
    pallas_call x1, Pallas kernels, local(): pl.pallas_call(functools.partial(kernel, n), out_shape=jax.ShapeDtypeStru...  54.7 us
    transpose x1, local copies, waits for them, and re-layouts, local(): jnp.transpose(out, (2, 1, 0, 3, 4)).reshape(STEPS, NX * n, LOCAL_HEADS, VH)  1.61 us

profile of v4, /device:TPU:1, one launch (start us, length us, event | category | flops | bytes accessed | tf_op | source)
XLA Modules:
  0.0 56.3 jit_solution(14260744858178699913)
XLA Ops:
  0.0 54.7 %shard_map.91 = bf16[4,8,16,128]{3,2,1,0:T(8,128)(2,1)} custom-call(s32[2]{0:T(128)} %length_hbm.1, bf16[4,1,4,512]{3,2,1,0:T(4,128)(2,1)} %ql_hbm.1, bf16[4,1,4,64]{3,2,1,0:T(4,128)(2,1)} %qr_hbm.1, s32[4,3,2,8]{3,2,1,0:T(2,128)} %bitcast.8, bf16[4,2,512]{2,1,0:T(2,128)(2,1)} %nl_hbm.1, bf16[4,2,64]{2,1,0:T(2,128)(2,1)} %nr_hbm.1, ...), custom_call_target="tpu_custom_call" | custom-call | tf_op jit(solution)/shard_map/pallas_call | solution.py:390
  54.7 1.6 %copy.10 = bf16[4,8,4,4,128]{4,3,2,1,0:T(4,128)(2,1)} copy(bf16[4,8,4,4,128]{4,3,0,1,2:T(4,128)(2,1)} %bitcast.6) | data formatting | bytes 262144 | tf_op jit(solution)/shard_map/transpose | solution.py:430

commit v5 on v4

--- a/solution.py
+++ b/solution.py
@@ -23,10 +23,18 @@
 FIRST = (((1,), (0,)), ((), ()))
 
 
+def mod(value, size):
+    return value % size if isinstance(value, int) else lax.rem(value, size)
+
+
+def div(value, size):
+    return value // size if isinstance(value, int) else lax.div(value, size)
+
+
 def column(x, core):
-    source_core = (x // 2 + core) % 2
+    source_core = mod(div(x, 2) + core, 2)
     source_x = x + source_core * (NX - 1 - 2 * x)
-    request = source_x % 2
+    request = mod(source_x, 2)
     return request, source_core, source_x
 
 
@@ -60,13 +68,13 @@
     length_hbm, ql_hbm, qr_hbm, sel_hbm, nl_hbm, nr_hbm, lat_hbm, rope_hbm, w_hbm,
     out_ref,
     length_ref, ql_ref, qr_ref, sel_ref, nl_ref, nr_ref, lat, rope, w, rows32, mine, q_all, keep,
-    part, part_in, joint, joint_in, done, done_in, gathered,
+    part, part_in, joint, joint_in, done, done_in, final,
     local_sem, q_send, q_recv, x_send, x_recv, px_send, px_recv, py_send, py_recv, back_sem,
-    oy_send, oy_recv, ox_send, ox_recv,
+    o_send, o_recv,
 ):
     b, c = lax.axis_index("batch"), lax.axis_index("ctx")
-    z, core = b // 2, b % 2
-    y, x = c // NX, c % NX
+    z, core = div(b, 2), mod(b, 2)
+    y, x = div(c, NX), mod(c, NX)
     far = n // 2
     few = max(1, n // 4)
     groups = n // few
@@ -80,37 +88,34 @@
         load.start()
 
     def at_y(step):
-        return (b, ((y + step + n) % n) * NX + x)
+        return (b, mod(y + step, n) * NX + x)
 
     def at_x(step):
-        return (b, y * NX + (x + step + NX) % NX)
+        return (b, y * NX + mod(x + step + NX, NX))
 
     request, source_core, source_x = column(x, core)
     own = request * 2 + source_core
     goal_x = x + core * (NX - 1 - 2 * x)
-    goal_column = (x % 2) * 2 + core
-    itself = (y == z) & (x // 2 == core) & (goal_x == x)
+    goal_column = mod(x, 2) * 2 + core
+    itself = (y == z) & (div(x, 2) == core) & (goal_x == x)
     other = jnp.logical_not(itself)
 
     def goal(step):
-        return (y * 2 + x // 2, ((y + step) % n) * NX + goal_x)
+        return (y * 2 + div(x, 2), mod(y + step, n) * NX + goal_x)
 
     def origin(step):
-        return (((z + step) % n) * 2 + source_core, z * NX + source_x)
+        return (mod(z + step, n) * 2 + source_core, z * NX + source_x)
 
     barrier = pltpu.get_barrier_semaphore()
 
     def greet(device):
         pl.semaphore_signal(barrier, inc=1, device_id=device, device_id_type=MESH)
 
-    @pl.loop(1, n)
-    def _(d):
+    for d in range(1, n):
         greet(goal(d))
         greet(origin(d))
         greet(at_y(d))
-
-    @pl.loop(1, NX)
-    def _(d):
+    for d in range(1, NX):
         greet(at_x(d))
 
     @pl.when(other)
@@ -135,7 +140,7 @@
         )
 
     def nearest(s):
-        return s % 2 * ((s + 1) // 2) + (1 - s % 2) * ((n - s // 2) % n)
+        return mod(s, 2) * div(s + 1, 2) + (1 - mod(s, 2)) * mod(n - div(s, 2), n)
 
     def q_copy(d):
         return remote(mine, q_all.at[goal_column, z], q_send.at[d], q_recv.at[z], goal(d))
@@ -144,8 +149,7 @@
         slot = q_all.at[own, k]
         remote(slot, slot, q_send.at[0], q_recv.at[k], goal(0)).wait_recv()
 
-    @pl.loop(1, n)
-    def _(s):
+    for s in range(1, n):
         q_copy(nearest(n - s)).start()
 
     @pl.when(other)
@@ -196,7 +200,7 @@
         load.wait()
 
     def px_copy(d, half):
-        target = column((x - d + NX) % NX, core)
+        target = column(mod(x - d + NX, NX), core)
         return remote(
             part.at[half, target[0] * 2 + target[1]], part_in.at[half, d - 1],
             px_send.at[d - 1, half], px_recv.at[d - 1, half], at_x(-d),
@@ -207,10 +211,10 @@
 
     @pl.loop(0, 2 * groups)
     def _(turn):
-        half = turn // 2
-        r = (request + 1 + turn) % 2
+        half = div(turn, 2)
+        r = mod(request + 1 + turn, 2)
         request_x = 2 * core + r
-        away = [(x - request_x - k * (NX - 1 - 2 * request_x) + 2 * NX) % NX for k in range(2)]
+        away = [mod(x - request_x - k * (NX - 1 - 2 * request_x) + 2 * NX, NX) for k in range(2)]
         for d in away:
             @pl.when(d > 0)
             def _():
@@ -258,7 +262,7 @@
             def _():
                 px_copy(d, half).start()
 
-    mine_k = (y + far) % n
+    mine_k = mod(y + far, n)
     q_own = q_all[own, mine_k].astype(jnp.float32)
     row_step = lax.broadcasted_iota(jnp.int32, (ROWS, 1), 0) // LOCAL_HEADS
     second = request.astype(jnp.float32)
@@ -277,7 +281,7 @@
         new_top = jnp.maximum(new_top, score)
 
     def py_copy(k):
-        to = (k + far) % n
+        to = mod(k + far, n)
         return remote(joint.at[k], joint_in.at[y], py_send.at[k], py_recv.at[y], (b, to * NX + x))
 
     @pl.loop(0, groups)
@@ -301,7 +305,7 @@
 
     @pl.loop(1, n)
     def _(d):
-        k = (y + d) % n
+        k = mod(y + d, n)
         remote(joint.at[0], joint_in.at[k], py_send.at[0], py_recv.at[k], at_y(d)).wait_recv()
 
     out, top, total = merged([joint_in[k] for k in range(n)], new_top)
@@ -311,7 +315,7 @@
         out = out + weight.astype(jnp.bfloat16).astype(jnp.float32) * new_rows[u]
     done[...] = out / total
 
-    back = remote(done, done_in, back_sem.at[0], back_sem.at[1], origin((mine_k - z + n) % n))
+    back = remote(done, done_in, back_sem.at[0], back_sem.at[1], origin(mod(mine_k - z + n, n)))
     back.start()
     loads[8].wait()
     back.wait_recv()
@@ -328,38 +332,39 @@
         product = lax.dot_general(terms, w[h], FIRST, preferred_element_type=jnp.float32)
         product = product[:ROWS] + (product[ROWS:2 * ROWS] + product[2 * ROWS:])
         result = jnp.where(row_head == h, product, result)
-    gathered[x, y] = result.astype(jnp.bfloat16)
-
-    def oy_copy(d):
-        slot = gathered.at[x, y]
-        return remote(slot, slot, oy_send.at[d - 1], oy_recv.at[d - 1], at_y(d))
-
-    def ox_copy(d):
-        return remote(gathered.at[x], out_ref.at[x], ox_send.at[d - 1], ox_recv.at[d - 1], at_x(d))
-
-    @pl.loop(1, n)
+    final[...] = result.astype(jnp.bfloat16)
+
+    def o_copy(dy, dx):
+        target = (b, mod(y + dy, n) * NX + mod(x + dx, NX))
+        return remote(final, out_ref.at[x, y], o_send.at[dx, dy], o_recv.at[dx, dy], target)
+
+    @pl.loop(0, n - 1)
     def _(s):
-        oy_copy(nearest(n - s)).start()
-
-    @pl.loop(1, n)
-    def _(d):
-        oy_copy(d).wait_recv()
-
-    for d in (2, 1, 3):
-        ox_copy(d).start()
-    keep_own = pltpu.make_async_copy(gathered.at[x], out_ref.at[x], local_sem.at[9])
+        dy = nearest(n - 1 - s)
+        for dx in (2, 1, 3, 0):
+            o_copy(dy, dx).start()
+
+    for dx in (2, 1, 3):
+        o_copy(0, dx).start()
+    keep_own = pltpu.make_async_copy(final, out_ref.at[x, y], local_sem.at[9])
     keep_own.start()
-    for d in (1, 3, 2):
-        ox_copy(d).wait_recv()
+
+    @pl.loop(1, n * NX)
+    def _(k):
+        o_copy(div(k, NX), mod(k, NX)).wait_recv()
+
     keep_own.wait()
+
+    @pl.loop(1, n * NX)
+    def _(k):
+        o_copy(div(k, NX), mod(k, NX)).wait_send()
 
     back.wait_send()
 
     @pl.loop(1, n)
     def _(d):
         q_copy(d).wait_send()
-        py_copy((mine_k + d) % n).wait_send()
-        oy_copy(d).wait_send()
+        py_copy(mod(mine_k + d, n)).wait_send()
 
     @pl.when(other)
     def _():
@@ -369,7 +374,6 @@
     def _(d):
         for half in range(groups):
             px_copy(d, half).wait_send()
-        ox_copy(d).wait_send()
 
         @pl.loop(0, n)
         def _(k):
@@ -412,15 +416,14 @@
             pltpu.VMEM((n, ROWS, WIDE), bf16),
             pltpu.VMEM((ROWS, KL), f32),
             pltpu.VMEM((ROWS, KL), f32),
-            pltpu.VMEM((NX, n, ROWS, VH), bf16),
+            pltpu.VMEM((ROWS, VH), bf16),
             dma((10,)),
             dma((n,)), dma((n,)),
             dma((NX - 1, n)), dma((NX - 1, n)),
             dma((NX - 1, n // few)), dma((NX - 1, n // few)),
             dma((n,)), dma((n,)),
             dma((2,)),
-            dma((n - 1,)), dma((n - 1,)),
-            dma((NX - 1,)), dma((NX - 1,)),
+            dma((NX, n)), dma((NX, n)),
         ],
         compiler_params=pltpu.CompilerParams(
             collective_id=0, has_side_effects=True, vmem_limit_bytes=60 * 1024 * 1024

time: 56.8 us -> 56.3 us (level)
  no operation moved by 1% of the time
where the time goes in v5:
time: 56.3 us; the launch traced here: 56.1 us
  Pallas kernels  54.5 us (97%)
  local copies, waits for them, and re-layouts  1.61 us (3%)
    pallas_call x1, Pallas kernels, local(): pl.pallas_call(functools.partial(kernel, n), out_shape=jax.ShapeDtypeStru...  54.5 us
    transpose x1, local copies, waits for them, and re-layouts, local(): jnp.transpose(out, (2, 1, 0, 3, 4)).reshape(STEPS, NX * n, LOCAL_HEADS, VH)  1.61 us

profile of v5, /device:TPU:1, one launch (start us, length us, event | category | flops | bytes accessed | tf_op | source)
XLA Modules:
  0.0 56.1 jit_solution(6394954101915969719)
XLA Ops:
  0.0 54.5 %shard_map.91 = bf16[4,8,16,128]{3,2,1,0:T(8,128)(2,1)} custom-call(s32[2]{0:T(128)} %length_hbm.1, bf16[4,1,4,512]{3,2,1,0:T(4,128)(2,1)} %ql_hbm.1, bf16[4,1,4,64]{3,2,1,0:T(4,128)(2,1)} %qr_hbm.1, s32[4,3,2,8]{3,2,1,0:T(2,128)} %bitcast.8, bf16[4,2,512]{2,1,0:T(2,128)(2,1)} %nl_hbm.1, bf16[4,2,64]{2,1,0:T(2,128)(2,1)} %nr_hbm.1, ...), custom_call_target="tpu_custom_call" | custom-call | tf_op jit(solution)/shard_map/pallas_call | solution.py:394
  54.5 1.6 %copy.10 = bf16[4,8,4,4,128]{4,3,2,1,0:T(4,128)(2,1)} copy(bf16[4,8,4,4,128]{4,3,0,1,2:T(4,128)(2,1)} %bitcast.6) | data formatting | bytes 262144 | tf_op jit(solution)/shard_map/transpose | solution.py:433

commit v6 on v5

--- a/solution.py
+++ b/solution.py
@@ -317,6 +317,25 @@
 
     back = remote(done, done_in, back_sem.at[0], back_sem.at[1], origin(mod(mine_k - z + n, n)))
     back.start()
+
+    @pl.loop(1, n)
+    def _(d):
+        q_copy(d).wait_send()
+        py_copy(mod(mine_k + d, n)).wait_send()
+
+    @pl.when(other)
+    def _():
+        q_copy(0).wait_send()
+
+    @pl.loop(1, NX)
+    def _(d):
+        for half in range(groups):
+            px_copy(d, half).wait_send()
+
+        @pl.loop(0, n)
+        def _(k):
+            x_copy(d, k).wait_send()
+
     loads[8].wait()
     back.wait_recv()
     value = done_in[...]
@@ -349,35 +368,17 @@
     keep_own = pltpu.make_async_copy(final, out_ref.at[x, y], local_sem.at[9])
     keep_own.start()
 
+    back.wait_send()
+
+    @pl.loop(1, n * NX)
+    def _(k):
+        o_copy(div(k, NX), mod(k, NX)).wait_send()
+
     @pl.loop(1, n * NX)
     def _(k):
         o_copy(div(k, NX), mod(k, NX)).wait_recv()
 
     keep_own.wait()
-
-    @pl.loop(1, n * NX)
-    def _(k):
-        o_copy(div(k, NX), mod(k, NX)).wait_send()
-
-    back.wait_send()
-
-    @pl.loop(1, n)
-    def _(d):
-        q_copy(d).wait_send()
-        py_copy(mod(mine_k + d, n)).wait_send()
-
-    @pl.when(other)
-    def _():
-        q_copy(0).wait_send()
-
-    @pl.loop(1, NX)
-    def _(d):
-        for half in range(groups):
-            px_copy(d, half).wait_send()
-
-        @pl.loop(0, n)
-        def _(k):
-            x_copy(d, k).wait_send()
 
 
 def local(

time: 56.3 us -> 55.6 us (0.988)
  Pallas kernels: 54.5 us -> 53.9 us
    pallas_call x1, Pallas kernels: 54.5 us -> 53.9 us  [local(): pl.pallas_call(functools.partial(kernel, n), out_shape=jax.ShapeDtypeStru...]
where the time goes in v6:
time: 55.6 us; the launch traced here: 55.5 us
  Pallas kernels  53.9 us (97%)
  local copies, waits for them, and re-layouts  1.61 us (3%)
    pallas_call x1, Pallas kernels, local(): pl.pallas_call(functools.partial(kernel, n), out_shape=jax.ShapeDtypeStru...  53.9 us
    transpose x1, local copies, waits for them, and re-layouts, local(): jnp.transpose(out, (2, 1, 0, 3, 4)).reshape(STEPS, NX * n, LOCAL_HEADS, VH)  1.61 us

profile of v6, /device:TPU:1, one launch (start us, length us, event | category | flops | bytes accessed | tf_op | source)
XLA Modules:
  0.0 55.5 jit_solution(7327410286323813291)
XLA Ops:
  0.0 53.9 %shard_map.91 = bf16[4,8,16,128]{3,2,1,0:T(8,128)(2,1)} custom-call(s32[2]{0:T(128)} %length_hbm.1, bf16[4,1,4,512]{3,2,1,0:T(4,128)(2,1)} %ql_hbm.1, bf16[4,1,4,64]{3,2,1,0:T(4,128)(2,1)} %qr_hbm.1, s32[4,3,2,8]{3,2,1,0:T(2,128)} %bitcast.8, bf16[4,2,512]{2,1,0:T(2,128)(2,1)} %nl_hbm.1, bf16[4,2,64]{2,1,0:T(2,128)(2,1)} %nr_hbm.1, ...), custom_call_target="tpu_custom_call" | custom-call | tf_op jit(solution)/shard_map/pallas_call | solution.py:395
  53.9 1.6 %copy.10 = bf16[4,8,4,4,128]{4,3,2,1,0:T(4,128)(2,1)} copy(bf16[4,8,4,4,128]{4,3,0,1,2:T(4,128)(2,1)} %bitcast.6) | data formatting | bytes 262144 | tf_op jit(solution)/shard_map/transpose | solution.py:434

commit v7 on v6

--- a/solution.py
+++ b/solution.py
@@ -296,6 +296,10 @@
             three = [stat[:, 3 * j:3 * j + 3] for stat in stats]
             k = half * few + j
             joint[k] = packed(*joined(values, three, None))
+
+        @pl.loop(0, few)
+        def _(j):
+            k = half * few + mod(j + y, few)
 
             @pl.when(k != mine_k)
             def _():

time: 55.6 us -> 56 us (level)
  no operation moved by 1% of the time
where the time goes in v7:
time: 56 us; the launch traced here: 55.9 us
  Pallas kernels  54.2 us (97%)
  local copies, waits for them, and re-layouts  1.61 us (3%)
    pallas_call x1, Pallas kernels, local(): pl.pallas_call(functools.partial(kernel, n), out_shape=jax.ShapeDtypeStru...  54.2 us
    transpose x1, local copies, waits for them, and re-layouts, local(): jnp.transpose(out, (2, 1, 0, 3, 4)).reshape(STEPS, NX * n, LOCAL_HEADS, VH)  1.61 us

profile of v7, /device:TPU:1, one launch (start us, length us, event | category | flops | bytes accessed | tf_op | source)
XLA Modules:
  0.0 55.9 jit_solution(15040405695082249461)
XLA Ops:
  0.0 54.2 %shard_map.91 = bf16[4,8,16,128]{3,2,1,0:T(8,128)(2,1)} custom-call(s32[2]{0:T(128)} %length_hbm.1, bf16[4,1,4,512]{3,2,1,0:T(4,128)(2,1)} %ql_hbm.1, bf16[4,1,4,64]{3,2,1,0:T(4,128)(2,1)} %qr_hbm.1, s32[4,3,2,8]{3,2,1,0:T(2,128)} %bitcast.8, bf16[4,2,512]{2,1,0:T(2,128)(2,1)} %nl_hbm.1, bf16[4,2,64]{2,1,0:T(2,128)(2,1)} %nr_hbm.1, ...), custom_call_target="tpu_custom_call" | custom-call | tf_op jit(solution)/shard_map/pallas_call | solution.py:399
  54.2 1.6 %copy.10 = bf16[4,8,4,4,128]{4,3,2,1,0:T(4,128)(2,1)} copy(bf16[4,8,4,4,128]{4,3,0,1,2:T(4,128)(2,1)} %bitcast.6) | data formatting | bytes 262144 | tf_op jit(solution)/shard_map/transpose | solution.py:438
